TPU v7x, 512 devices: a whole 4x8x8 slice. The times are simulated.
512 devices in a mesh: seq: 128 (over z, y, core), pair: 4 (over x).
Axes of the slice: x: 4, y: 8, z: 8, core: 2. Of those that a mesh axis runs over, the one named last changes fastest.
Arguments:
- query_rows: bfloat16 [65536, 2560], P(('seq', 'pair')), may hold values from -6 to 6
- key_rows: bfloat16 [65536, 2560], P(('seq', 'pair')), may hold values from -6 to 6
- value_rows: bfloat16 [65536, 2560], P(('seq', 'pair')), may hold values from -6 to 6
- grad_out: bfloat16 [65536, 2560], P(('seq', 'pair')), may hold values from -24 to 24
- log_sum_exp: float32 [20, 65536], P(None, ('seq', 'pair')), may hold values from 0 to 10, as said below
- row_delta: float32 [20, 65536], P(None, ('seq', 'pair')), may hold values from -18 to 18
- block_counts: int32 [512], P(('seq', 'pair')), may hold values from 1 to 4, as said below
Outputs:
- grad_query: bfloat16 [65536, 2560], P(('seq', 'pair'))
- grad_key: bfloat16 [65536, 2560], P(('seq', 'pair'))
- grad_value: bfloat16 [65536, 2560], P(('seq', 'pair'))
Inputs may be any that keep to these rules, and one draw needn't show every extreme that they name: block_counts[0] is 1, and every later entry is either 1 (a document starts there) or one more than the entry before it; the first 4 entries and the last 4 entries are 1, 2, ... up to 4. `log_sum_exp`: each entry lies within one half of ln(m) + 0.5, m the number of positions that row is allowed to attend.
All inputs are finite; a program needn't handle non-finite values.
Results may differ from a plain program's by a relative error of at most 0.0056.
Values may be sent and summed in bfloat16 or wider, within the bound.
A program may use at most 64 MiB of HBM per device.

v0:
```python
import jax
import jax.numpy as jnp
from jax import lax
from jax.sharding import PartitionSpec as P

REACH = 4


def from_behind(value, axis, by):
    peers = lax.axis_size(axis)
    pairs = [(i, i + by) for i in range(peers) if 0 <= i + by < peers]
    return lax.ppermute(value, axis, pairs)


def from_behind_2(block, axis, distance):
    devices = range(lax.axis_size(axis))
    route = [((i - distance) % len(devices), i) for i in devices]
    return lax.ppermute(block, axis, route)


def tile_terms(
    query_blk,
    grad_blk,
    lse_blk,
    delta_blk,
    key_blk,
    value_blk,
    row_offset,
    col_offset,
    row_limit,
    block_rows,
):
    head_count = lse_blk.shape[0]
    head_width = query_blk.shape[1] // head_count
    scaling = head_width ** (-0.5)
    query_total = query_blk.shape[0]
    key_total = key_blk.shape[0]
    query_heads = query_blk.reshape(query_total, head_count, head_width)
    grad_heads = grad_blk.reshape(query_total, head_count, head_width)
    key_heads = key_blk.reshape(key_total, head_count, head_width)
    value_heads = value_blk.reshape(key_total, head_count, head_width)
    scores = (
        jnp.einsum("qhe,khe->hqk", query_heads, key_heads, preferred_element_type=jnp.float32)
        * scaling
    )
    distance_grid = row_offset[:, None] + col_offset[None, :]
    row_place = jnp.arange(query_total, dtype=jnp.int32) % block_rows
    col_place = jnp.arange(key_total, dtype=jnp.int32) % block_rows
    allowed = (distance_grid < row_limit[:, None]) & (
        (distance_grid > 0) | (row_place[:, None] >= col_place[None, :])
    )
    attention = jnp.where(allowed[None], jnp.exp(scores - lse_blk[:, :, None]), 0.0)
    attention_half = attention.astype(jnp.bfloat16)
    value_grad = jnp.einsum(
        "hqk,qhe->khe", attention_half, grad_heads, preferred_element_type=jnp.float32
    )
    dprobs = jnp.einsum("qhe,khe->hqk", grad_heads, value_heads, preferred_element_type=jnp.float32)
    dscores = (attention * (dprobs - delta_blk[:, :, None]) * scaling).astype(jnp.bfloat16)
    query_grad = jnp.einsum("hqk,khe->qhe", dscores, key_heads, preferred_element_type=jnp.float32)
    key_grad = jnp.einsum("hqk,qhe->khe", dscores, query_heads, preferred_element_type=jnp.float32)
    return (
        query_grad.reshape(query_total, -1),
        key_grad.reshape(key_total, -1),
        value_grad.reshape(key_total, -1),
    )


def shards(query_rows, key_rows, value_rows, grad_out, log_sum_exp, row_delta, block_counts):
    block_rows = query_rows.shape[0]
    total_width = query_rows.shape[1]
    zero_offsets = jnp.zeros((block_rows,), jnp.int32)
    zero_grad = jnp.zeros((block_rows, total_width), jnp.float32)
    own_limit = jnp.broadcast_to(block_counts[0], (block_rows,))
    moving = (key_rows, value_rows)
    carried = (zero_grad, zero_grad)
    query_grad = zero_grad
    for distance in range(REACH):
        if distance > 0:
            moving = from_behind((moving[0], moving[1]), ("seq", "pair"), 1)
            carried = from_behind_2((carried[0], carried[1]), ("seq", "pair"), 1)
        col_offsets = jnp.full((block_rows,), distance, jnp.int32)
        query_part, key_part, value_part = tile_terms(
            query_rows,
            grad_out,
            log_sum_exp,
            row_delta,
            moving[0],
            moving[1],
            zero_offsets,
            col_offsets,
            own_limit,
            block_rows,
        )
        query_grad = query_grad + query_part
        carried = (carried[0] + key_part, carried[1] + value_part)
    key_grad, value_grad = (
        from_behind_2(carried[0].astype(jnp.bfloat16), ("seq", "pair"), 1 - REACH).astype(
            jnp.float32
        ),
        from_behind_2(carried[1].astype(jnp.bfloat16), ("seq", "pair"), 1 - REACH).astype(
            jnp.float32
        ),
    )
    return (
        query_grad.astype(jnp.bfloat16),
        key_grad.astype(jnp.bfloat16),
        value_grad.astype(jnp.bfloat16),
    )


def solution(mesh):
    return jax.shard_map(
        shards,
        mesh=mesh,
        in_specs=(
            P(("seq", "pair"), None),
            P(("seq", "pair"), None),
            P(("seq", "pair"), None),
            P(("seq", "pair"), None),
            P(None, ("seq", "pair")),
            P(None, ("seq", "pair")),
            P(("seq", "pair")),
        ),
        out_specs=(P(("seq", "pair"), None), P(("seq", "pair"), None), P(("seq", "pair"), None)),
        check_vma=False,
    )
```

profile of v0, /device:TPU:506, one launch (start us, length us, event | category | flops | bytes accessed | tf_op | source)
XLA Modules:
  0.0 299.0 jit_solution(9039387692816437958)
XLA Ops:
  0.7 2.3 copy.42
  2.9 3.4 %collective-permute-start = (bf16[128,2560]{0,1:T(8,128)(2,1)}, bf16[128,2560]{0,1:T(8,128)(2,1)}, u32[]{:S(2)}, u32[]{:S(2)}) collective-permute-start(bf16[128,2560]{0,1:T(8,128)(2,1)} %copy.42), channel_id=1, source_target_pairs={{0,1},{1,2},{2,3},{3,4},{4,5},{5,6},{6,7},{7,8},{8,9},{9,10},{10,1... | collective-permute-start | bytes 1966088 | tf_op jit(solution)/shard_map/ppermute | solution.py:12
  6.3 0.3 copy.41
  7.4 0.3 copy.45
  7.7 1.1 copy.46
  8.8 0.1 compare_and_fusion
  8.9 1.8 fusion.19
  10.7 0.7 fusion.20
  11.4 1.4 fusion.34
  12.8 2.8 copy.63
  15.6 3.1 %collective-permute-start.6 = (f32[128,2560]{1,0:T(8,128)}, f32[128,2560]{1,0:T(8,128)}, u32[]{:S(2)}, u32[]{:S(2)}) collective-permute-start(f32[128,2560]{1,0:T(8,128)} %copy.63), channel_id=1, source_target_pairs={{511,0},{0,1},{1,2},{2,3},{3,4},{4,5},{5,6},{6,7},{7,8},{8,9},{9,1... | collective-permute-start | bytes 3932168 | tf_op jit(solution)/shard_map/ppermute | solution.py:18
  18.7 1.9 collective-permute-start.1
  20.6 1.4 fusion.31
  22.0 2.8 copy.67
  24.8 3.0 %collective-permute-start.10 = (f32[128,2560]{1,0:T(8,128)}, f32[128,2560]{1,0:T(8,128)}, u32[]{:S(2)}, u32[]{:S(2)}) collective-permute-start(f32[128,2560]{1,0:T(8,128)} %copy.67), channel_id=1, source_target_pairs={{511,0},{0,1},{1,2},{2,3},{3,4},{4,5},{5,6},{6,7},{7,8},{8,9},{9,1... | collective-permute-start | bytes 3932168 | tf_op jit(solution)/shard_map/ppermute | solution.py:18
  27.8 1.7 fusion.14
  29.6 3.1 %collective-permute-start.2 = (bf16[128,2560]{0,1:T(8,128)(2,1)}, bf16[128,2560]{0,1:T(8,128)(2,1)}, u32[]{:S(2)}, u32[]{:S(2)}) collective-permute-start(bf16[128,2560]{0,1:T(8,128)(2,1)} %collective-permute-done), channel_id=1, source_target_pairs={{0,1},{1,2},{2,3},{3,4},{4,5},{5,6},{6,7},{7,8},{8,9},{9,10},{10,1... | collective-permute-start | bytes 1966088 | tf_op jit(solution)/shard_map/ppermute | solution.py:12
  32.7 32.2 %collective-permute-done.1 = bf16[128,2560]{0,1:T(8,128)(2,1)} collective-permute-done((bf16[128,2560]{0,1:T(8,128)(2,1)}, bf16[128,2560]{0,1:T(8,128)(2,1)}, u32[]{:S(2)}, u32[]{:S(2)}) %collective-permute-start.1) | collective-permute-done | bytes 655392 | tf_op jit(solution)/shard_map/ppermute | solution.py:12
  64.9 1.7 fusion.21
  66.6 1.4 fusion.35
  68.0 2.8 copy.64
  70.8 5.8 %collective-permute-start.3 = (bf16[128,2560]{0,1:T(8,128)(2,1)}, bf16[128,2560]{0,1:T(8,128)(2,1)}, u32[]{:S(2)}, u32[]{:S(2)}) collective-permute-start(bf16[128,2560]{0,1:T(8,128)(2,1)} %collective-permute-done.1), channel_id=1, source_target_pairs={{0,1},{1,2},{2,3},{3,4},{4,5},{5,6},{6,7},{7,8},{8,9},{9,10},{10,1... | collective-permute-start | bytes 1966088 | tf_op jit(solution)/shard_map/ppermute | solution.py:12
  76.6 2.9 add.59
  79.6 54.4 %collective-permute-start.7 = (f32[128,2560]{1,0:T(8,128)}, f32[128,2560]{1,0:T(8,128)}, u32[]{:S(2)}, u32[]{:S(2)}) collective-permute-start(f32[128,2560]{1,0:T(8,128)} %add.59), channel_id=1, source_target_pairs={{511,0},{0,1},{1,2},{2,3},{3,4},{4,5},{5,6},{6,7},{7,8},{8,9},{9,1... | collective-permute-start | bytes 3932168 | tf_op jit(solution)/shard_map/ppermute | solution.py:18
  133.9 2.7 fusion.33
  136.7 1.4 fusion.29
  138.1 1.7 copy.68
  139.8 2.6 add.62
  142.4 5.0 %collective-permute-start.11 = (f32[128,2560]{1,0:T(8,128)}, f32[128,2560]{1,0:T(8,128)}, u32[]{:S(2)}, u32[]{:S(2)}) collective-permute-start(f32[128,2560]{1,0:T(8,128)} %add.62), channel_id=1, source_target_pairs={{511,0},{0,1},{1,2},{2,3},{3,4},{4,5},{5,6},{6,7},{7,8},{8,9},{9,1... | collective-permute-start | bytes 3932168 | tf_op jit(solution)/shard_map/ppermute | solution.py:18
  147.4 1.9 collective-permute-start.4
  149.4 1.7 fusion.9
  151.1 1.7 fusion.22
  152.9 1.9 collective-permute-start.5
  154.8 1.4 fusion.36
  156.2 2.9 copy.65
  159.1 4.4 %collective-permute-done.7 = f32[128,2560]{1,0:T(8,128)} collective-permute-done((f32[128,2560]{1,0:T(8,128)}, f32[128,2560]{1,0:T(8,128)}, u32[]{:S(2)}, u32[]{:S(2)}) %collective-permute-start.7) | collective-permute-done | bytes 1310752 | tf_op jit(solution)/shard_map/ppermute | solution.py:18
  163.5 3.0 %add.60 = f32[128,2560]{1,0:T(8,128)} add(f32[128,2560]{1,0:T(8,128)} %collective-permute-done.7, f32[128,2560]{1,0:T(8,128)} %copy.65) | non-fusion elementwise | flops 327680 | bytes 3932160 | tf_op jit(solution)/shard_map/add | solution.py:95
  166.5 11.3 %collective-permute-start.8 = (f32[128,2560]{1,0:T(8,128)}, f32[128,2560]{1,0:T(8,128)}, u32[]{:S(2)}, u32[]{:S(2)}) collective-permute-start(f32[128,2560]{1,0:T(8,128)} %add.60), channel_id=1, source_target_pairs={{511,0},{0,1},{1,2},{2,3},{3,4},{4,5},{5,6},{6,7},{7,8},{8,9},{9,1... | collective-permute-start | bytes 3932168 | tf_op jit(solution)/shard_map/ppermute | solution.py:18
  177.8 1.4 fusion.27
  179.2 2.8 copy.69
  182.0 23.6 %collective-permute-done.4 = bf16[128,2560]{0,1:T(8,128)(2,1)S(1)} collective-permute-done((bf16[128,2560]{0,1:T(8,128)(2,1)}, bf16[128,2560]{0,1:T(8,128)(2,1)S(1)}, u32[]{:S(2)}, u32[]{:S(2)}) %collective-permute-start.4) | collective-permute-done | bytes 655392 | tf_op jit(solution)/shard_map/ppermute | solution.py:12
  205.6 0.8 copy-done.8
  206.4 1.7 fusion.4
  208.2 9.0 %collective-permute-done.5 = bf16[128,2560]{0,1:T(8,128)(2,1)} collective-permute-done((bf16[128,2560]{0,1:T(8,128)(2,1)}, bf16[128,2560]{0,1:T(8,128)(2,1)}, u32[]{:S(2)}, u32[]{:S(2)}) %collective-permute-start.5) | collective-permute-done | bytes 655392 | tf_op jit(solution)/shard_map/ppermute | solution.py:12
  217.2 1.8 fusion.23
  219.1 2.6 add.63
  221.7 13.5 %collective-permute-start.12 = (f32[128,2560]{1,0:T(8,128)}, f32[128,2560]{1,0:T(8,128)}, u32[]{:S(2)}, u32[]{:S(2)}) collective-permute-start(f32[128,2560]{1,0:T(8,128)} %add.63), channel_id=1, source_target_pairs={{511,0},{0,1},{1,2},{2,3},{3,4},{4,5},{5,6},{6,7},{7,8},{8,9},{9,1... | collective-permute-start | bytes 3932168 | tf_op jit(solution)/shard_map/ppermute | solution.py:18
  235.2 1.4 fusion.37
  236.6 2.8 copy.66
  239.4 1.4 fusion.25
  240.8 1.8 copy.70
  242.6 7.3 %collective-permute-done.8 = f32[128,2560]{1,0:T(8,128)} collective-permute-done((f32[128,2560]{1,0:T(8,128)}, f32[128,2560]{1,0:T(8,128)}, u32[]{:S(2)}, u32[]{:S(2)}) %collective-permute-start.8) | collective-permute-done | bytes 1310752 | tf_op jit(solution)/shard_map/ppermute | solution.py:18
  250.0 2.3 add_convert_fusion.1
  252.3 2.0 collective-permute-start.9
  254.3 26.1 %collective-permute-done.12 = f32[128,2560]{1,0:T(8,128)} collective-permute-done((f32[128,2560]{1,0:T(8,128)}, f32[128,2560]{1,0:T(8,128)}, u32[]{:S(2)}, u32[]{:S(2)}) %collective-permute-start.12) | collective-permute-done | bytes 1310752 | tf_op jit(solution)/shard_map/ppermute | solution.py:18
  280.4 2.3 add_convert_fusion
  282.7 2.0 collective-permute-start.13
  284.8 1.7 convolution_add_fusion.2
  286.5 1.7 convolution_add_fusion.1
  288.2 0.6 fusion.24
  288.8 1.1 copy.71
  289.9 7.5 %collective-permute-done.13 = bf16[128,2560]{1,0:T(8,128)(2,1)S(1)} collective-permute-done((bf16[128,2560]{1,0:T(8,128)(2,1)}, bf16[128,2560]{1,0:T(8,128)(2,1)S(1)}, u32[]{:S(2)}, u32[]{:S(2)}) %collective-permute-start.13) | collective-permute-done | bytes 655392 | tf_op jit(solution)/shard_map/ppermute | solution.py:18
  297.4 0.8 copy.91
  298.2 0.8 copy.92
  (37 shorter events, 0.1 us)
Async XLA Ops:
  0.6 5.7 %copy-start.10 = (bf16[128,2560]{1,0:T(8,128)(2,1)S(1)}, bf16[128,2560]{1,0:T(8,128)(2,1)}, u32[]{:S(2)}) copy-start(bf16[128,2560]{1,0:T(8,128)(2,1)} %param.7) | copy-start | bytes 1966084
  0.6 6.7 %copy-start.11 = (bf16[128,2560]{1,0:T(8,128)(2,1)S(1)}, bf16[128,2560]{1,0:T(8,128)(2,1)}, u32[]{:S(2)}) copy-start(bf16[128,2560]{1,0:T(8,128)(2,1)} %param.10) | copy-start | bytes 1966084
  2.9 24.9 %collective-permute-start = (bf16[128,2560]{0,1:T(8,128)(2,1)}, bf16[128,2560]{0,1:T(8,128)(2,1)}, u32[]{:S(2)}, u32[]{:S(2)}) collective-permute-start(bf16[128,2560]{0,1:T(8,128)(2,1)} %copy.42), channel_id=1, source_target_pairs={{0,1},{1,2},{2,3},{3,4},{4,5},{5,6},{6,7},{7,8},{8,9},{9,10},{10,1... | collective-permute-start | bytes 1966088 | tf_op jit(solution)/shard_map/ppermute | solution.py:12
  6.3 1.3 copy-start.12
  7.3 1.5 copy-start.14
  8.9 1.8 copy-start.7
  8.9 1.8 copy-start.13
  15.6 61.1 %collective-permute-start.6 = (f32[128,2560]{1,0:T(8,128)}, f32[128,2560]{1,0:T(8,128)}, u32[]{:S(2)}, u32[]{:S(2)}) collective-permute-start(f32[128,2560]{1,0:T(8,128)} %copy.63), channel_id=1, source_target_pairs={{511,0},{0,1},{1,2},{2,3},{3,4},{4,5},{5,6},{6,7},{7,8},{8,9},{9,1... | collective-permute-start | bytes 3932168 | tf_op jit(solution)/shard_map/ppermute | solution.py:18
  18.7 46.2 %collective-permute-start.1 = (bf16[128,2560]{0,1:T(8,128)(2,1)}, bf16[128,2560]{0,1:T(8,128)(2,1)}, u32[]{:S(2)}, u32[]{:S(2)}) collective-permute-start(bf16[128,2560]{0,1:T(8,128)(2,1)} %copy.46), channel_id=1, source_target_pairs={{0,1},{1,2},{2,3},{3,4},{4,5},{5,6},{6,7},{7,8},{8,9},{9,10},{10,1... | collective-permute-start | bytes 1966088 | tf_op jit(solution)/shard_map/ppermute | solution.py:12
  24.8 115.0 %collective-permute-start.10 = (f32[128,2560]{1,0:T(8,128)}, f32[128,2560]{1,0:T(8,128)}, u32[]{:S(2)}, u32[]{:S(2)}) collective-permute-start(f32[128,2560]{1,0:T(8,128)} %copy.67), channel_id=1, source_target_pairs={{511,0},{0,1},{1,2},{2,3},{3,4},{4,5},{5,6},{6,7},{7,8},{8,9},{9,1... | collective-permute-start | bytes 3932168 | tf_op jit(solution)/shard_map/ppermute | solution.py:18
  29.6 117.8 %collective-permute-start.2 = (bf16[128,2560]{0,1:T(8,128)(2,1)}, bf16[128,2560]{0,1:T(8,128)(2,1)}, u32[]{:S(2)}, u32[]{:S(2)}) collective-permute-start(bf16[128,2560]{0,1:T(8,128)(2,1)} %collective-permute-done), channel_id=1, source_target_pairs={{0,1},{1,2},{2,3},{3,4},{4,5},{5,6},{6,7},{7,8},{8,9},{9,10},{10,1... | collective-permute-start | bytes 1966088 | tf_op jit(solution)/shard_map/ppermute | solution.py:12
  66.6 1.4 copy-start
  70.8 80.3 %collective-permute-start.3 = (bf16[128,2560]{0,1:T(8,128)(2,1)}, bf16[128,2560]{0,1:T(8,128)(2,1)}, u32[]{:S(2)}, u32[]{:S(2)}) collective-permute-start(bf16[128,2560]{0,1:T(8,128)(2,1)} %collective-permute-done.1), channel_id=1, source_target_pairs={{0,1},{1,2},{2,3},{3,4},{4,5},{5,6},{6,7},{7,8},{8,9},{9,10},{10,1... | collective-permute-start | bytes 1966088 | tf_op jit(solution)/shard_map/ppermute | solution.py:12
  79.6 83.9 %collective-permute-start.7 = (f32[128,2560]{1,0:T(8,128)}, f32[128,2560]{1,0:T(8,128)}, u32[]{:S(2)}, u32[]{:S(2)}) collective-permute-start(f32[128,2560]{1,0:T(8,128)} %add.59), channel_id=1, source_target_pairs={{511,0},{0,1},{1,2},{2,3},{3,4},{4,5},{5,6},{6,7},{7,8},{8,9},{9,1... | collective-permute-start | bytes 3932168 | tf_op jit(solution)/shard_map/ppermute | solution.py:18
  142.4 76.7 %collective-permute-start.11 = (f32[128,2560]{1,0:T(8,128)}, f32[128,2560]{1,0:T(8,128)}, u32[]{:S(2)}, u32[]{:S(2)}) collective-permute-start(f32[128,2560]{1,0:T(8,128)} %add.62), channel_id=1, source_target_pairs={{511,0},{0,1},{1,2},{2,3},{3,4},{4,5},{5,6},{6,7},{7,8},{8,9},{9,1... | collective-permute-start | bytes 3932168 | tf_op jit(solution)/shard_map/ppermute | solution.py:18
  147.4 58.2 %collective-permute-start.4 = (bf16[128,2560]{0,1:T(8,128)(2,1)}, bf16[128,2560]{0,1:T(8,128)(2,1)S(1)}, u32[]{:S(2)}, u32[]{:S(2)}) collective-permute-start(bf16[128,2560]{0,1:T(8,128)(2,1)} %collective-permute-done.2), channel_id=1, source_target_pairs={{0,1},{1,2},{2,3},{3,4},{4,5},{5,6},{6,7},{7,8},{8,9},{9,10},{10,1... | collective-permute-start | bytes 1966088 | tf_op jit(solution)/shard_map/ppermute | solution.py:12
  152.9 1.9 copy-start.2
  152.9 64.3 %collective-permute-start.5 = (bf16[128,2560]{0,1:T(8,128)(2,1)}, bf16[128,2560]{0,1:T(8,128)(2,1)}, u32[]{:S(2)}, u32[]{:S(2)}) collective-permute-start(bf16[128,2560]{0,1:T(8,128)(2,1)} %collective-permute-done.3), channel_id=1, source_target_pairs={{0,1},{1,2},{2,3},{3,4},{4,5},{5,6},{6,7},{7,8},{8,9},{9,10},{10,1... | collective-permute-start | bytes 1966088 | tf_op jit(solution)/shard_map/ppermute | solution.py:12
  166.5 83.5 %collective-permute-start.8 = (f32[128,2560]{1,0:T(8,128)}, f32[128,2560]{1,0:T(8,128)}, u32[]{:S(2)}, u32[]{:S(2)}) collective-permute-start(f32[128,2560]{1,0:T(8,128)} %add.60), channel_id=1, source_target_pairs={{511,0},{0,1},{1,2},{2,3},{3,4},{4,5},{5,6},{6,7},{7,8},{8,9},{9,1... | collective-permute-start | bytes 3932168 | tf_op jit(solution)/shard_map/ppermute | solution.py:18
  205.6 0.8 copy-start.8
  217.2 1.9 copy-start.6
  221.7 58.7 %collective-permute-start.12 = (f32[128,2560]{1,0:T(8,128)}, f32[128,2560]{1,0:T(8,128)}, u32[]{:S(2)}, u32[]{:S(2)}) collective-permute-start(f32[128,2560]{1,0:T(8,128)} %add.63), channel_id=1, source_target_pairs={{511,0},{0,1},{1,2},{2,3},{3,4},{4,5},{5,6},{6,7},{7,8},{8,9},{9,1... | collective-permute-start | bytes 3932168 | tf_op jit(solution)/shard_map/ppermute | solution.py:18
  240.8 9.1 %copy-start.4 = (f32[128,2560]{1,0:T(8,128)S(1)}, f32[128,2560]{1,0:T(8,128)}, u32[]{:S(2)}) copy-start(f32[128,2560]{1,0:T(8,128)} %copy.66) | copy-start | bytes 3932164
  252.3 32.5 %copy-start.1 = (bf16[20,128,128]{2,1,0:T(8,128)(2,1)S(1)}, bf16[20,128,128]{2,1,0:T(8,128)(2,1)}, u32[]{:S(2)}) copy-start(bf16[20,128,128]{2,1,0:T(8,128)(2,1)} %copy-done) | copy-start | bytes 1966084
  252.3 32.5 %copy-start.5 = (f32[20,128,128]{1,2,0:T(8,128)S(1)}, f32[20,128,128]{1,2,0:T(8,128)}, u32[]{:S(2)}) copy-start(f32[20,128,128]{1,2,0:T(8,128)} %fusion.33) | copy-start | bytes 3932164
  252.3 37.6 %collective-permute-start.9 = (bf16[128,2560]{1,0:T(8,128)(2,1)}, bf16[128,2560]{1,0:T(8,128)(2,1)S(1)}, u32[]{:S(2)}, u32[]{:S(2)}) collective-permute-start(bf16[128,2560]{1,0:T(8,128)(2,1)} %add_convert_fusion.1), channel_id=1, source_target_pairs={{3,0},{4,1},{5,2},{6,3},{7,4},{8,5},{9,6},{10,7},{11,8},{12,9},{13... | collective-permute-start | bytes 1966088 | tf_op jit(solution)/shard_map/ppermute | solution.py:18
  282.7 3.7 %copy-start.3 = (bf16[20,128,128]{2,1,0:T(8,128)(2,1)S(1)}, bf16[20,128,128]{2,1,0:T(8,128)(2,1)}, u32[]{:S(2)}) copy-start(bf16[20,128,128]{2,1,0:T(8,128)(2,1)} %copy-done.2) | copy-start | bytes 1966084
  282.7 14.6 %collective-permute-start.13 = (bf16[128,2560]{1,0:T(8,128)(2,1)}, bf16[128,2560]{1,0:T(8,128)(2,1)S(1)}, u32[]{:S(2)}, u32[]{:S(2)}) collective-permute-start(bf16[128,2560]{1,0:T(8,128)(2,1)} %add_convert_fusion), channel_id=1, source_target_pairs={{3,0},{4,1},{5,2},{6,3},{7,4},{8,5},{9,6},{10,7},{11,8},{12,9},{13... | collective-permute-start | bytes 1966088 | tf_op jit(solution)/shard_map/ppermute | solution.py:18
  286.5 1.7 copy-start.9
where the time goes:
time: 300 us; the launch traced here: 299 us
  starting transfers between devices  112 us (37%)
  waiting for transfers between devices  110 us (37%)
  matrix products  30.9 us (10%)
  local copies, waits for them, and re-layouts  28.1 us (9%)
  other arithmetic  15.8 us (5%)
    ppermute x8, starting transfers between devices, from_behind_2(): return lax.ppermute(block, axis, route)  94.4 us
    ppermute x6, waiting for transfers between devices, from_behind(): return lax.ppermute(value, axis, pairs)  64.8 us
    ppermute x8, waiting for transfers between devices, from_behind_2(): return lax.ppermute(block, axis, route)  45.3 us
    ppermute x6, starting transfers between devices, from_behind(): return lax.ppermute(value, axis, pairs)  18.1 us
    reshape x4, local copies, waits for them, and re-layouts, tile_terms(): key_grad.reshape(key_total, -1)  11.3 us
    add x4, other arithmetic, shards(): carried = (carried[0] + key_part, carried[1] + value_part)  11.1 us
    reshape x4, local copies, waits for them, and re-layouts, tile_terms(): value_grad.reshape(key_total, -1)  9.13 us
    unnamed x37, local copies, waits for them, and re-layouts  7.65 us
  transfers between devices with their start and end apart: 14, of which 7 were waited for; matrix products, arithmetic and copies ran while one was open for 23% of the time, Pallas kernels for 0%

commit v1 on v0

v1 whole, which is shorter than its diff:
```python
import functools
import math

import jax
import jax.numpy as jnp
from jax import lax
from jax.experimental import pallas as pl
from jax.experimental.pallas import tpu as pltpu
from jax.sharding import PartitionSpec as P

MESH = pl.DeviceIdType.MESH
BLK = 128
DIM = 128
RING = 4
HALO = 3
LOG2E = math.log2(math.e)
NEVER = 1e30
NT = (((1,), (1,)), ((), ()))
TN = (((0,), (0,)), ((), ()))


def dot(a, b, dims=(((1,), (0,)), ((), ()))):
    return lax.dot_general(a, b, dims, preferred_element_type=jnp.float32)


def kernel(
    groups,
    per,
    q_hbm,
    k_hbm,
    v_hbm,
    g_hbm,
    lse_ref,
    delta_ref,
    cnt_ref,
    dq_hbm,
    dk_hbm,
    dv_hbm,
    in_buf,
    own_stats,
    stats,
    out_buf,
    ds_buf,
    in_send,
    in_recv,
    in_local_sem,
    halo_send,
    halo_recv,
    stat_send,
    stat_recv,
    stat_halo_send,
    stat_halo_recv,
    out_send,
    out_recv,
    out_local_sem,
):
    s = lax.axis_index("seq")
    x = lax.axis_index("pair")
    after = lax.rem(s + 1, groups)
    before = lax.rem(s + groups - 1, groups)
    scale = DIM ** (-0.5)

    own_stats[...] = jnp.zeros_like(own_stats)
    for c in range(RING):
        own_stats[c, 0:per] = lse_ref[c * per : (c + 1) * per, :] * LOG2E
        own_stats[c, per : 2 * per] = delta_ref[c * per : (c + 1) * per, :]
        own_stats[c, 2 * per : 2 * per + 1] = jnp.full((1, BLK), cnt_ref[0], jnp.int32).astype(
            jnp.float32
        )

    barrier = pltpu.get_barrier_semaphore()
    for d in range(1, RING):
        pl.semaphore_signal(
            barrier, 1, device_id=(s, lax.rem(x + d, RING)), device_id_type=MESH
        )
    pl.semaphore_signal(barrier, 1, device_id=(after, x), device_id_type=MESH)
    pl.semaphore_signal(barrier, 1, device_id=(before, x), device_id_type=MESH)
    pl.semaphore_wait(barrier, RING + 1)

    def cols(owner, j):
        return pl.ds(pl.multiple_of((owner * per + j) * DIM, DIM), DIM)

    sources = (k_hbm, v_hbm, q_hbm, g_hbm)
    first = (HALO, HALO, 0, 0)
    outs = (dq_hbm, dk_hbm, dv_hbm)

    def copy_to(src, dst, send, recv, device):
        return pltpu.make_async_remote_copy(
            src_ref=src,
            dst_ref=dst,
            send_sem=send,
            recv_sem=recv,
            device_id=device,
            device_id_type=MESH,
        )

    def covers(ref, send, recv):
        return copy_to(ref, ref, send, recv, (after, x))

    def in_copy(i, j, there):
        return copy_to(
            sources[i].at[:, cols(there, j)],
            in_buf.at[j, i, first[i] + x],
            in_send,
            in_recv.at[j],
            (s, there),
        )

    def in_local(i, j):
        return pltpu.make_async_copy(
            sources[i].at[:, cols(x, j)], in_buf.at[j, i, first[i] + x], in_local_sem.at[j]
        )

    def stat_copy(there):
        return copy_to(own_stats.at[there], stats.at[x], stat_send, stat_recv, (s, there))

    def halo_copies(j):
        to_after = [
            copy_to(
                in_buf.at[j, i, pl.ds(RING, HALO)],
                in_buf.at[j, i, pl.ds(0, HALO)],
                halo_send,
                halo_recv.at[j],
                (after, x),
            )
            for i in (0, 1)
        ]
        to_before = [
            copy_to(
                in_buf.at[j, i, pl.ds(0, HALO)],
                in_buf.at[j, i, pl.ds(RING, HALO)],
                halo_send,
                halo_recv.at[j],
                (before, x),
            )
            for i in (2, 3)
        ]
        return to_after + to_before

    stat_halo = copy_to(
        stats.at[pl.ds(0, HALO)],
        stats.at[pl.ds(RING, HALO)],
        stat_halo_send,
        stat_halo_recv,
        (before, x),
    )

    def out_copy(i, j, there):
        return copy_to(
            out_buf.at[j, i, there],
            outs[i].at[:, cols(x, j)],
            out_send,
            out_recv,
            (s, there),
        )

    def out_local(i, j):
        return pltpu.make_async_copy(
            out_buf.at[j, i, x], outs[i].at[:, cols(x, j)], out_local_sem
        )

    for d in range(1, RING):
        stat_copy(lax.rem(x + d, RING)).start()

    def send_inputs(j, carry):
        for d in (2, 1, 3):
            for i in range(4):
                in_copy(i, j, lax.rem(x + d, RING)).start()
        for i in range(4):
            in_local(i, j).start()
        return carry

    lax.fori_loop(0, per, send_inputs, 0)
    stats[x] = own_stats[x]
    covers(stats.at[pl.ds(0, RING - 1)], stat_send, stat_recv).wait_recv()
    stat_halo.start()

    def compute(j):
        row = lax.broadcasted_iota(jnp.int32, (BLK, BLK), 0)
        col = lax.broadcasted_iota(jnp.int32, (BLK, BLK), 1)
        causal = col >= row
        for a in range(RING + HALO):
            low = max(a - HALO, 0)
            high = a + 1
            blocks = high - low
            keys = in_buf[j, 0, a]
            values = in_buf[j, 1, a]
            queries = in_buf[j, 2, low:high].reshape(blocks * BLK, DIM)
            grads = in_buf[j, 3, low:high].reshape(blocks * BLK, DIM)
            scores = dot(keys, queries, NT)
            dprobs = dot(values, grads, NT)
            halves, dscores = [], []
            for n in range(blocks):
                b = low + n
                distance = b - (a - HALO)
                distance = -distance if distance < 0 else distance
                tile = slice(n * BLK, (n + 1) * BLK)
                gap = b + HALO - a
                lse = stats[b, pl.ds(j, 1), :]
                delta = stats[b, pl.ds(per + j, 1), :]
                count = stats[b, 2 * per : 2 * per + 1, :]
                lse = jnp.where(count > gap, lse, NEVER)
                prob = jnp.exp2(scores[:, tile] * (scale * LOG2E) - lse)
                if gap == 0:
                    prob = jnp.where(causal, prob, 0.0)
                dscore = (prob * (dprobs[:, tile] - delta) * scale).astype(jnp.bfloat16)
                if b < RING:
                    ds_buf[b, (a - b) * BLK : (a - b + 1) * BLK, :] = dscore
                if a >= HALO:
                    halves.append(prob.astype(jnp.bfloat16))
                    dscores.append(dscore)
            if a >= HALO:
                half = jnp.concatenate(halves, axis=1)
                dscore = jnp.concatenate(dscores, axis=1)
                out_buf[j, 1, a - HALO] = dot(dscore, queries).astype(jnp.bfloat16)
                out_buf[j, 2, a - HALO] = dot(half, grads).astype(jnp.bfloat16)
        for b in range(RING):
            keys = in_buf[j, 0, b : b + RING].reshape(RING * BLK, DIM)
            out_buf[j, 0, b] = dot(ds_buf[b], keys, TN).astype(jnp.bfloat16)

    def step(j, carry):
        @pl.when(j < per)
        def _():
            covers(in_buf.at[j, :, pl.ds(0, RING - 1)], in_send, in_recv.at[j]).wait_recv()
            here = in_buf.at[j, :, 0]
            pltpu.make_async_copy(here, here, in_local_sem.at[j]).wait()
            for copy in halo_copies(j):
                copy.start()

        @pl.when(j > 0)
        def _():
            i = j - 1

            @pl.when(i == 0)
            def _():
                stat_halo.wait_recv()

            covers(in_buf.at[i, :, pl.ds(0, HALO)], halo_send, halo_recv.at[i]).wait_recv()
            compute(i)
            for d in (2, 1, 3):
                for n in range(3):
                    out_copy(n, i, lax.rem(x + d, RING)).start()
            for n in range(3):
                out_local(n, i).start()

        return carry

    lax.fori_loop(0, per + 1, step, 0)

    covers(stats.at[pl.ds(0, RING - 1)], stat_send, stat_recv).wait_send()
    stat_halo.wait_send()
    inputs = in_buf.at[:, :, pl.ds(0, RING - 1)]
    covers(inputs, in_send, in_recv.at[0]).wait_send()
    covers(inputs, halo_send, halo_recv.at[0]).wait_send()
    results = out_buf.at[:, :, pl.ds(0, RING - 1)]
    covers(results, out_send, out_recv).wait_send()
    covers(results, out_send, out_recv).wait_recv()
    own = out_buf.at[:, :, 0]
    pltpu.make_async_copy(own, own, out_local_sem).wait()


def shards(groups, q, k, v, g, lse, delta, counts):
    heads = lse.shape[0]
    per = heads // RING
    rows, width = q.shape
    hbm = pl.BlockSpec(memory_space=pl.ANY)
    vmem = pl.BlockSpec(memory_space=pltpu.VMEM)
    grad = jax.ShapeDtypeStruct((rows, width), jnp.bfloat16)
    return pl.pallas_call(
        functools.partial(kernel, groups, per),
        out_shape=(grad, grad, grad),
        in_specs=[hbm] * 4 + [vmem] * 2 + [pl.BlockSpec(memory_space=pltpu.SMEM)],
        out_specs=(hbm, hbm, hbm),
        scratch_shapes=[
            pltpu.VMEM((per, 4, RING + HALO, BLK, DIM), jnp.bfloat16),
            pltpu.VMEM((RING, 16, BLK), jnp.float32),
            pltpu.VMEM((RING + HALO, 16, BLK), jnp.float32),
            pltpu.VMEM((per, 3, RING, BLK, DIM), jnp.bfloat16),
            pltpu.VMEM((RING, RING * BLK, BLK), jnp.bfloat16),
            pltpu.SemaphoreType.DMA,
            pltpu.SemaphoreType.DMA((per,)),
            pltpu.SemaphoreType.DMA((per,)),
            pltpu.SemaphoreType.DMA,
            pltpu.SemaphoreType.DMA((per,)),
            pltpu.SemaphoreType.DMA,
            pltpu.SemaphoreType.DMA,
            pltpu.SemaphoreType.DMA,
            pltpu.SemaphoreType.DMA,
            pltpu.SemaphoreType.DMA,
            pltpu.SemaphoreType.DMA,
            pltpu.SemaphoreType.DMA,
        ],
        compiler_params=pltpu.CompilerParams(
            collective_id=0, has_side_effects=True, vmem_limit_bytes=40 << 20
        ),
        cost_estimate=pl.CostEstimate(
            flops=184 * per * BLK * BLK * DIM,
            bytes_accessed=14 * rows * width,
            transcendentals=22 * per * BLK * BLK,
        ),
    )(q, k, v, g, lse, delta, counts)


def solution(mesh):
    groups = mesh.shape["seq"]
    rows = P(("seq", "pair"), None)
    cols = P(None, ("seq", "pair"))
    return jax.shard_map(
        functools.partial(shards, groups),
        mesh=mesh,
        in_specs=(rows, rows, rows, rows, cols, cols, P(("seq", "pair"))),
        out_specs=(rows, rows, rows),
        check_vma=False,
    )
```

time: 300 us -> 68 us (0.23)
  the two profiles are of different devices: /device:TPU:506 before, /device:TPU:2 now
where the time goes in v1:
time: 68 us; the launch traced here: 67.6 us
  Pallas kernels  58 us (85%)
  local copies, waits for them, and re-layouts  8.26 us (12%)
  between operations  1.3 us (2%)
    pallas_call x1, Pallas kernels, shards(): pl.pallas_call(functools.partial(kernel, groups, per), out_shape=(grad, g...  58 us
    unnamed x15, local copies, waits for them, and re-layouts  8.26 us

profile of v1, /device:TPU:2, one launch (start us, length us, event | category | flops | bytes accessed | tf_op | source)
XLA Modules:
  0.0 67.6 jit_solution(14044312737181154256)
XLA Ops:
  1.3 0.0 copy-start
  1.3 1.1 %copy-done = bf16[128,2560]{1,0:T(8,128)(2,1)S(1)} copy-done((bf16[128,2560]{1,0:T(8,128)(2,1)S(1)}, bf16[128,2560]{1,0:T(8,128)(2,1)}, u32[]{:S(2)}) %copy-start) | copy-done | bytes 655384
  2.4 0.0 copy-start.1
  2.4 1.1 %copy-done.1 = bf16[128,2560]{1,0:T(8,128)(2,1)S(1)} copy-done((bf16[128,2560]{1,0:T(8,128)(2,1)S(1)}, bf16[128,2560]{1,0:T(8,128)(2,1)}, u32[]{:S(2)}) %copy-start.1) | copy-done | bytes 655384
  3.5 0.0 copy-start.2
  3.5 1.1 %copy-done.2 = bf16[128,2560]{1,0:T(8,128)(2,1)S(1)} copy-done((bf16[128,2560]{1,0:T(8,128)(2,1)S(1)}, bf16[128,2560]{1,0:T(8,128)(2,1)}, u32[]{:S(2)}) %copy-start.2) | copy-done | bytes 655384
  4.5 0.0 copy-start.3
  4.5 1.1 %copy-done.3 = bf16[128,2560]{1,0:T(8,128)(2,1)S(1)} copy-done((bf16[128,2560]{1,0:T(8,128)(2,1)S(1)}, bf16[128,2560]{1,0:T(8,128)(2,1)}, u32[]{:S(2)}) %copy-start.3) | copy-done | bytes 655384
  5.6 0.0 copy-start.4
  5.6 0.7 %copy-done.4 = f32[20,128]{1,0:T(8,128)S(1)} copy-done((f32[20,128]{1,0:T(8,128)S(1)}, f32[20,128]{1,0:T(8,128)}, u32[]{:S(2)}) %copy-start.4) | copy-done | bytes 10264
  6.3 0.0 copy-start.5
  6.3 0.7 %copy-done.5 = f32[20,128]{1,0:T(8,128)S(1)} copy-done((f32[20,128]{1,0:T(8,128)S(1)}, f32[20,128]{1,0:T(8,128)}, u32[]{:S(2)}) %copy-start.5) | copy-done | bytes 10264
  7.0 58.0 %shard_map.94 = (bf16[128,2560]{1,0:T(8,128)(2,1)S(1)}, bf16[128,2560]{1,0:T(8,128)(2,1)S(1)}, bf16[128,2560]{1,0:T(8,128)(2,1)S(1)}) custom-call(bf16[128,2560]{1,0:T(8,128)(2,1)S(1)} %copy-done, bf16[128,2560]{1,0:T(8,128)(2,1)S(1)} %copy-done.1, bf16[128,2560]{1,0:T(8,128)(2,1)S(1)} %copy-done.2, bf16[128,2560]{1,0:T(8,128)(2,1)S(1)} %copy-done.3, ...), custom_call_target="tpu_custom_call" | custom-call | flops 1929379840 | bytes 4587520 | tf_op jit(solution)/shard_map/pallas_call | solution.py:269
  65.0 0.8 %copy.14 = bf16[128,2560]{1,0:T(8,128)(2,1)} copy(bf16[128,2560]{1,0:T(8,128)(2,1)S(1)} %get-tuple-element.6) | data formatting | bytes 1310720
  65.9 0.8 %copy.15 = bf16[128,2560]{1,0:T(8,128)(2,1)} copy(bf16[128,2560]{1,0:T(8,128)(2,1)S(1)} %get-tuple-element.7) | data formatting | bytes 1310720
  66.7 0.8 %copy.16 = bf16[128,2560]{1,0:T(8,128)(2,1)} copy(bf16[128,2560]{1,0:T(8,128)(2,1)S(1)} %get-tuple-element.8) | data formatting | bytes 1310720
Async XLA Ops:
  1.3 1.1 %copy-start = (bf16[128,2560]{1,0:T(8,128)(2,1)S(1)}, bf16[128,2560]{1,0:T(8,128)(2,1)}, u32[]{:S(2)}) copy-start(bf16[128,2560]{1,0:T(8,128)(2,1)} %q_hbm.1) | copy-start | bytes 1966084
  2.4 1.1 %copy-start.1 = (bf16[128,2560]{1,0:T(8,128)(2,1)S(1)}, bf16[128,2560]{1,0:T(8,128)(2,1)}, u32[]{:S(2)}) copy-start(bf16[128,2560]{1,0:T(8,128)(2,1)} %k_hbm.1) | copy-start | bytes 1966084
  3.5 1.1 %copy-start.2 = (bf16[128,2560]{1,0:T(8,128)(2,1)S(1)}, bf16[128,2560]{1,0:T(8,128)(2,1)}, u32[]{:S(2)}) copy-start(bf16[128,2560]{1,0:T(8,128)(2,1)} %v_hbm.1) | copy-start | bytes 1966084
  4.5 1.1 %copy-start.3 = (bf16[128,2560]{1,0:T(8,128)(2,1)S(1)}, bf16[128,2560]{1,0:T(8,128)(2,1)}, u32[]{:S(2)}) copy-start(bf16[128,2560]{1,0:T(8,128)(2,1)} %g_hbm.1) | copy-start | bytes 1966084
  5.6 0.7 %copy-start.4 = (f32[20,128]{1,0:T(8,128)S(1)}, f32[20,128]{1,0:T(8,128)}, u32[]{:S(2)}) copy-start(f32[20,128]{1,0:T(8,128)} %lse_ref.1) | copy-start | bytes 30724
  6.3 0.7 %copy-start.5 = (f32[20,128]{1,0:T(8,128)S(1)}, f32[20,128]{1,0:T(8,128)}, u32[]{:S(2)}) copy-start(f32[20,128]{1,0:T(8,128)} %delta_ref.1) | copy-start | bytes 30724

commit v2 on v1

--- a/solution.py
+++ b/solution.py
@@ -30,12 +30,18 @@
     k_hbm,
     v_hbm,
     g_hbm,
-    lse_ref,
-    delta_ref,
+    lse_hbm,
+    delta_hbm,
     cnt_ref,
     dq_hbm,
     dk_hbm,
     dv_hbm,
+    lse_ref,
+    delta_ref,
+    q_ref,
+    k_ref,
+    v_ref,
+    g_ref,
     in_buf,
     own_stats,
     stats,
@@ -53,6 +59,7 @@
     out_send,
     out_recv,
     out_local_sem,
+    row_sem,
 ):
     s = lax.axis_index("seq")
     x = lax.axis_index("pair")
@@ -60,13 +67,16 @@
     before = lax.rem(s + groups - 1, groups)
     scale = DIM ** (-0.5)
 
-    own_stats[...] = jnp.zeros_like(own_stats)
-    for c in range(RING):
-        own_stats[c, 0:per] = lse_ref[c * per : (c + 1) * per, :] * LOG2E
-        own_stats[c, per : 2 * per] = delta_ref[c * per : (c + 1) * per, :]
-        own_stats[c, 2 * per : 2 * per + 1] = jnp.full((1, BLK), cnt_ref[0], jnp.int32).astype(
-            jnp.float32
-        )
+    fetches = [
+        pltpu.make_async_copy(lse_hbm, lse_ref, row_sem.at[0]),
+        pltpu.make_async_copy(delta_hbm, delta_ref, row_sem.at[1]),
+        pltpu.make_async_copy(k_hbm, k_ref, row_sem.at[2]),
+        pltpu.make_async_copy(v_hbm, v_ref, row_sem.at[3]),
+        pltpu.make_async_copy(q_hbm, q_ref, row_sem.at[4]),
+        pltpu.make_async_copy(g_hbm, g_ref, row_sem.at[5]),
+    ]
+    for fetch in fetches:
+        fetch.start()
 
     barrier = pltpu.get_barrier_semaphore()
     for d in range(1, RING):
@@ -80,7 +90,7 @@
     def cols(owner, j):
         return pl.ds(pl.multiple_of((owner * per + j) * DIM, DIM), DIM)
 
-    sources = (k_hbm, v_hbm, q_hbm, g_hbm)
+    sources = (k_ref, v_ref, q_ref, g_ref)
     first = (HALO, HALO, 0, 0)
     outs = (dq_hbm, dk_hbm, dv_hbm)
 
@@ -159,8 +169,21 @@
             out_buf.at[j, i, x], outs[i].at[:, cols(x, j)], out_local_sem
         )
 
+    for fetch in fetches[:2]:
+        fetch.wait()
+    own_stats[...] = jnp.zeros_like(own_stats)
+    for c in range(RING):
+        own_stats[c, 0:per] = lse_ref[c * per : (c + 1) * per, :] * LOG2E
+        own_stats[c, per : 2 * per] = delta_ref[c * per : (c + 1) * per, :]
+        own_stats[c, 2 * per : 2 * per + 1] = jnp.full((1, BLK), cnt_ref[0], jnp.int32).astype(
+            jnp.float32
+        )
     for d in range(1, RING):
         stat_copy(lax.rem(x + d, RING)).start()
+    stats[x] = own_stats[x]
+
+    for fetch in fetches[2:]:
+        fetch.wait()
 
     def send_inputs(j, carry):
         for d in (2, 1, 3):
@@ -171,7 +194,6 @@
         return carry
 
     lax.fori_loop(0, per, send_inputs, 0)
-    stats[x] = own_stats[x]
     covers(stats.at[pl.ds(0, RING - 1)], stat_send, stat_recv).wait_recv()
     stat_halo.start()
 
@@ -259,6 +281,17 @@
     pltpu.make_async_copy(own, own, out_local_sem).wait()
 
 
+def keep(a, b, c, a_out, b_out, c_out, sems):
+    copies = [
+        pltpu.make_async_copy(src, dst, sems.at[i])
+        for i, (src, dst) in enumerate(((a, a_out), (b, b_out), (c, c_out)))
+    ]
+    for copy in copies:
+        copy.start()
+    for copy in copies:
+        copy.wait()
+
+
 def shards(groups, q, k, v, g, lse, delta, counts):
     heads = lse.shape[0]
     per = heads // RING
@@ -266,12 +299,18 @@
     hbm = pl.BlockSpec(memory_space=pl.ANY)
     vmem = pl.BlockSpec(memory_space=pltpu.VMEM)
     grad = jax.ShapeDtypeStruct((rows, width), jnp.bfloat16)
-    return pl.pallas_call(
+    grads = pl.pallas_call(
         functools.partial(kernel, groups, per),
         out_shape=(grad, grad, grad),
-        in_specs=[hbm] * 4 + [vmem] * 2 + [pl.BlockSpec(memory_space=pltpu.SMEM)],
-        out_specs=(hbm, hbm, hbm),
+        in_specs=[hbm] * 6 + [pl.BlockSpec(memory_space=pltpu.SMEM)],
+        out_specs=(vmem, vmem, vmem),
         scratch_shapes=[
+            pltpu.VMEM(lse.shape, jnp.float32),
+            pltpu.VMEM(delta.shape, jnp.float32),
+            pltpu.VMEM((rows, width), jnp.bfloat16),
+            pltpu.VMEM((rows, width), jnp.bfloat16),
+            pltpu.VMEM((rows, width), jnp.bfloat16),
+            pltpu.VMEM((rows, width), jnp.bfloat16),
             pltpu.VMEM((per, 4, RING + HALO, BLK, DIM), jnp.bfloat16),
             pltpu.VMEM((RING, 16, BLK), jnp.float32),
             pltpu.VMEM((RING + HALO, 16, BLK), jnp.float32),
@@ -289,9 +328,10 @@
             pltpu.SemaphoreType.DMA,
             pltpu.SemaphoreType.DMA,
             pltpu.SemaphoreType.DMA,
+            pltpu.SemaphoreType.DMA((6,)),
         ],
         compiler_params=pltpu.CompilerParams(
-            collective_id=0, has_side_effects=True, vmem_limit_bytes=40 << 20
+            collective_id=0, has_side_effects=True, vmem_limit_bytes=123 << 19
         ),
         cost_estimate=pl.CostEstimate(
             flops=184 * per * BLK * BLK * DIM,
@@ -299,6 +339,16 @@
             transcendentals=22 * per * BLK * BLK,
         ),
     )(q, k, v, g, lse, delta, counts)
+    return pl.pallas_call(
+        keep,
+        out_shape=(grad, grad, grad),
+        in_specs=[vmem] * 3,
+        out_specs=(hbm, hbm, hbm),
+        scratch_shapes=[pltpu.SemaphoreType.DMA((3,))],
+        cost_estimate=pl.CostEstimate(
+            flops=0, bytes_accessed=6 * rows * width, transcendentals=0
+        ),
+    )(*grads)
 
 
 def solution(mesh):

time: 68 us -> 63.6 us (0.935)
  local copies, waits for them, and re-layouts: 8.26 us -> 0 us
  Pallas kernels: 58 us -> 62.1 us
    unnamed x15 -> x0, local copies, waits for them, and re-layouts: 8.26 us -> none
    pallas_call x0 -> x1, Pallas kernels: none -> 2.78 us  [shards(): pl.pallas_call(keep, out_shape=(grad, grad, grad), in_specs=[vmem] * 3, o...]
    pallas_call x1, Pallas kernels: 58 us -> 59.3 us  [shards(): pl.pallas_call(functools.partial(kernel, groups, per), out_shape=(grad, g...]
where the time goes in v2:
time: 63.6 us; the launch traced here: 63.4 us
  Pallas kernels  62.1 us (98%)
  between operations  1.29 us (2%)
    pallas_call x1, Pallas kernels, shards(): pl.pallas_call(functools.partial(kernel, groups, per), out_shape=(grad, g...  59.3 us
    pallas_call x1, Pallas kernels, shards(): pl.pallas_call(keep, out_shape=(grad, grad, grad), in_specs=[vmem] * 3, o...  2.78 us

profile of v2, /device:TPU:2, one launch (start us, length us, event | category | flops | bytes accessed | tf_op | source)
XLA Modules:
  0.0 63.4 jit_solution(6458716352835379773)
XLA Ops:
  1.3 59.3 %shard_map.94 = (bf16[128,2560]{1,0:T(8,128)(2,1)}, bf16[128,2560]{1,0:T(8,128)(2,1)}, bf16[128,2560]{1,0:T(8,128)(2,1)}) custom-call(bf16[128,2560]{1,0:T(8,128)(2,1)} %q_hbm.1, bf16[128,2560]{1,0:T(8,128)(2,1)} %k_hbm.1, bf16[128,2560]{1,0:T(8,128)(2,1)} %v_hbm.1, bf16[128,2560]{1,0:T(8,128)(2,1)} %g_hbm.1, f32[20,128]{1,0:T(8,128)} %lse_hbm.1, ...), custom_call_target="tpu_custom_call" | custom-call | flops 1929379840 | bytes 4587520 | tf_op jit(solution)/shard_map/pallas_call | solution.py:302
  60.6 2.8 %shard_map.95 = (bf16[128,2560]{1,0:T(8,128)(2,1)}, bf16[128,2560]{1,0:T(8,128)(2,1)}, bf16[128,2560]{1,0:T(8,128)(2,1)}) custom-call(bf16[128,2560]{1,0:T(8,128)(2,1)} %get-tuple-element.6.a, bf16[128,2560]{1,0:T(8,128)(2,1)} %get-tuple-element.7.b, bf16[128,2560]{1,0:T(8,128)(2,1)} %get-tuple-element.8.c), custom_call_target="tpu_custom_call" | custom-call | bytes 1966080 | tf_op jit(solution)/shard_map/pallas_call | solution.py:342

commit v3 on v0

v3 whole, which is shorter than its diff:
```python
import functools
import math

import jax
import jax.numpy as jnp
from jax import lax
from jax.experimental import pallas as pl
from jax.experimental.pallas import tpu as pltpu
from jax.sharding import PartitionSpec as P

MESH = pl.DeviceIdType.MESH
BLK = 128
DIM = 128
RING = 4
LOG2E = math.log2(math.e)
NEVER = 1e30
NN = (((1,), (0,)), ((), ()))
NT = (((1,), (1,)), ((), ()))
TN = (((0,), (0,)), ((), ()))
FWD, BACK = 4, 5


def dot(a, b, dims=NN):
    return lax.dot_general(a, b, dims, preferred_element_type=jnp.float32)


def either(flags):
    total = flags[0]
    for flag in flags[1:]:
        total = jnp.logical_or(total, flag)
    return total


def both(a, b):
    return jnp.logical_and(a, b)


def kernel(
    blocks,
    heads,
    q_hbm,
    k_hbm,
    v_hbm,
    g_hbm,
    lse_hbm,
    delta_hbm,
    cnt_ref,
    dq_ref,
    dk_ref,
    dv_ref,
    q_own,
    k_own,
    v_own,
    g_own,
    kv_far,
    qg_far,
    stats,
    counts,
    send_f,
    send_b,
    got_f,
    got_b,
    far_f,
    far_b,
    acc,
    part,
    fetch_sem,
    count_send,
    count_recv,
    stat_send,
    stat_recv,
    pre_send,
    pre_recv,
    f_send,
    f_recv,
    b_send,
    b_recv,
    far_send,
    far_recv,
):
    periods = heads // 4
    x = lax.axis_index("pair")
    me = lax.axis_index("seq") * RING + x
    scale = DIM ** (-0.5)

    def at(offset):
        there = lax.rem(me + (offset + blocks), blocks)
        return (lax.div(there, RING), lax.rem(there, RING))

    def remote(src, dst, send, recv, offset):
        return pltpu.make_async_remote_copy(
            src_ref=src,
            dst_ref=dst,
            send_sem=send,
            recv_sem=recv,
            device_id=at(offset),
            device_id_type=MESH,
        )

    fetches = [
        pltpu.make_async_copy(lse_hbm, stats.at[0, pl.ds(0, heads)], fetch_sem.at[0]),
        pltpu.make_async_copy(delta_hbm, stats.at[0, pl.ds(heads, heads)], fetch_sem.at[1]),
        pltpu.make_async_copy(k_hbm, k_own, fetch_sem.at[2]),
        pltpu.make_async_copy(v_hbm, v_own, fetch_sem.at[3]),
        pltpu.make_async_copy(q_hbm, q_own, fetch_sem.at[4]),
        pltpu.make_async_copy(g_hbm, g_own, fetch_sem.at[5]),
    ]
    for fetch in fetches:
        fetch.start()
    counts[0] = jnp.full((8, BLK), cnt_ref[0], jnp.int32).astype(jnp.float32)

    barrier = pltpu.get_barrier_semaphore()
    for offset in (-1, 1, 2, 3, -3, -4, 4):
        pl.semaphore_signal(barrier, 1, device_id=at(offset), device_id_type=MESH)
    pl.semaphore_wait(barrier, 7)

    count_copies = [
        remote(counts.at[0], counts.at[i], count_send.at[i], count_recv.at[i], -i)
        for i in (1, 2, 3)
    ]
    for copy in count_copies:
        copy.start()

    stat_copies = [
        remote(stats.at[0], stats.at[i], stat_send.at[i], stat_recv.at[i], offset)
        for i, offset in ((1, -1), (2, 1), (3, -3))
    ]

    for fetch in fetches[:2]:
        fetch.wait()
    for copy in stat_copies:
        copy.start()

    def wide(k, first):
        return pl.ds(pl.multiple_of((4 * k + first) * DIM, 2 * DIM), 2 * DIM)

    def pre_copy(i, k):
        own = (k_own, v_own, q_own, g_own)[i]
        src = own.at[:, wide(k, 0 if i < 2 else 2)]
        dst = (kv_far if i < 2 else qg_far).at[k, i % 2]
        return remote(src, dst, pre_send.at[i, k], pre_recv.at[i, k], 4 if i < 2 else -4)

    def start_pre(k):
        for i in range(4):
            pre_copy(i, k).start()

    for fetch in fetches[2:]:
        fetch.wait()
    start_pre(0)
    place = cnt_ref[0]
    p0, p1, p2, p3 = (place == i for i in (1, 2, 3, 4))

    def cols(k, i):
        return pl.ds(pl.multiple_of((4 * k + i) * DIM, DIM), DIM)

    def content(kind, i, k, side):
        if kind == "kv":
            return (k_own, v_own)[side][:, cols(k, i)]
        if kind == "qg":
            return (q_own, g_own)[side][:, cols(k, i)]
        if kind == "kvx":
            return kv_far[k, side, :, i * DIM : (i + 1) * DIM]
        if kind == "qgx":
            return qg_far[k, side, :, (i - 2) * DIM : (i - 1) * DIM]
        if kind == "dkv":
            return part[k - 1, i, 1 + side]
        return part[k - 1, i + side, 0]

    def fwd_copy(k, s):
        return remote(send_f.at[k, s], got_f.at[k, s], f_send.at[k, s], f_recv.at[k, s], 1)

    def back_copy(k, s):
        return remote(send_b.at[k, s], got_b.at[k, s], b_send.at[k, s], b_recv.at[k, s], -1)

    def far_copy(k, i):
        if i == 0:
            src, dst = got_f.at[k, pl.ds(2, 2)], far_f.at[k]
        else:
            src, dst = got_b.at[k, 4], far_b.at[k]
        return remote(src, dst, far_send.at[k, i], far_recv.at[k, i], -4 if i == 0 else 4)

    def direct_copy(i):
        if i == 0:
            src, dst = part.at[periods - 1, pl.ds(0, 2), pl.ds(1, 2)], far_f.at[periods]
        else:
            src, dst = part.at[periods - 1, pl.ds(2, 2), 0], far_b.at[periods]
        at_end = (far_send.at[periods, i], far_recv.at[periods, i])
        return remote(src, dst, *at_end, -3 if i == 0 else 3)

    def send(table, k, s, back, ins=True, outs=True):
        stage = send_b if back else send_f
        table = [e for e in table if (ins and e[1][0] != "d") or (outs and e[1][0] == "d")]
        for side in range(2):
            value = content(table[-1][1], table[-1][2], k, side)
            for flag, kind, i in table[:-1]:
                value = jnp.where(flag, content(kind, i, k, side), value)
            stage[k, s, side] = value
        (back_copy if back else fwd_copy)(k, s).start()

    def wait_pre(k, which):
        for i in which:
            pre_copy(i, k).wait_recv()

    send(((p1, "kv", 3), (None, "qg", 2)), 0, 2, True)
    send(((None, "qg", 3),), 0, 3, True)
    start_pre(1)
    wait_pre(0, (0, 1))
    for s in range(2):
        send(((p0, "kvx", s), (None, "qg", s)), 0, s, True)

    for copy in count_copies:
        copy.wait_recv()
    c1, c2, c3 = (jnp.max(counts[i]) for i in (1, 2, 3))
    p0l4 = both(p0, c3 == 4.0)
    p1l4 = both(p1, c2 == 4.0)
    p2l4 = both(p2, c1 == 4.0)
    p0s = both(both(p0, c1 == 2.0), c3 != 4.0)
    p1s = both(p1, c2 != 4.0)
    p1g3 = both(p1, c1 == 3.0)
    p1l3 = both(p1g3, c2 != 4.0)
    p2l3 = both(p2, c1 != 4.0)
    last = c1 == 1.0

    fwd_table = (
        ((p0l4, "kv", 2), (either([p0s, p1l4]), "kv", 0), (p2l4, "qg", 0), (last, "qgx", 2)),
        ((p0l4, "kv", 3), (either([p0s, p1l4]), "kv", 1), (p2l4, "qg", 1), (last, "qgx", 3)),
        (
            (either([p0s, p1l4]), "kv", 2),
            (either([p0l4, p1l3, p2l4]), "dq", 0),
            (p3, "dkv", 0),
        ),
        (
            (p0s, "kv", 3),
            (p0l4, "dkv", 3),
            (either([p1g3, p2l4]), "dq", 2),
            (p3, "dkv", 1),
        ),
    )
    back_table = (
        ((p0, "kvx", 0), (either([p2l4, p1s]), "dkv", 0), (None, "qg", 0)),
        ((p0, "kvx", 1), (either([p2l4, p1s]), "dkv", 1), (None, "qg", 1)),
        ((p1, "kv", 3), (None, "qg", 2)),
        ((p1, "dkv", 2), (None, "qg", 3)),
        ((p1, "dkv", 3), (p2l4, "dkv", 2), (p3, "dq", 0), (None, "dq", 2)),
    )

    def post(k, s, back, ins=True, outs=True):
        send((back_table if back else fwd_table)[s], k, s, back, ins, outs)

    row = lax.broadcasted_iota(jnp.int32, (BLK, BLK), 0)
    col = lax.broadcasted_iota(jnp.int32, (BLK, BLK), 1)
    causal = col >= row

    has_k = (either([p3, p2l4, p1s]),) * 2 + (either([p1, p2l4]), either([p0l4, p1]))
    has_q = (either([p0l4, p2l4, p3, p1l3]),) * 2 + (either([p0l4, p1g3, p2l4]),) * 2
    own_q_far_k = (has_k[0], has_k[1], p1, p1)
    far_q_own_k = (both(has_q[0], jnp.logical_not(p3)),) * 2 + (has_q[2], has_q[3])

    def compute(k, i):
        f = [got_f.at[k, s] for s in range(FWD)]
        b = [got_b.at[k, s] for s in range(BACK)]

        def far_kv(side):
            if i < 2:
                value = jnp.where(p3, b[i][side], f[i][side])
            elif i == 2:
                value = jnp.where(p1l4, f[0][side], f[2][side])
            else:
                value = jnp.where(p1l4, f[1][side], f[3][side])
                value = jnp.where(p0, b[2][side], value)
            return jnp.where(has_k[i], value, jnp.zeros_like(value))

        def far_qg(side):
            if i < 2:
                value = jnp.where(p3, f[i][side], b[i][side])
            else:
                value = jnp.where(p0, f[i - 2][side], b[i][side])
            return jnp.where(has_q[i], value, jnp.zeros_like(value))

        here = cols(k, i)
        keys = jnp.concatenate([k_own[:, here], far_kv(0)], axis=0)
        values = jnp.concatenate([v_own[:, here], far_kv(1)], axis=0)
        queries = jnp.concatenate([q_own[:, here], far_qg(0)], axis=0)
        grads = jnp.concatenate([g_own[:, here], far_qg(1)], axis=0)
        h = 4 * k + i
        lse_row, delta_row = pl.ds(h, 1), pl.ds(heads + h, 1)

        def far_row(at_row):
            if i < 2:
                return jnp.where(p3, stats[2, at_row, :], stats[1, at_row, :])
            return jnp.where(p0, stats[3, at_row, :], stats[1, at_row, :])

        lse = [stats[0, lse_row, :] * LOG2E, far_row(lse_row) * LOG2E]
        delta = [stats[0, delta_row, :], far_row(delta_row)]
        scores = dot(keys, queries, NT)
        dprobs = dot(values, grads, NT)
        halves, dscores = [], []
        for u in range(2):
            for t in range(2):
                shift = lse[t]
                if u or t:
                    allowed = (
                        both(has_k[i], has_q[i])
                        if u and t
                        else (own_q_far_k[i] if u else far_q_own_k[i])
                    )
                    shift = jnp.where(allowed, shift, jnp.full_like(shift, NEVER))
                tile = (slice(u * BLK, (u + 1) * BLK), slice(t * BLK, (t + 1) * BLK))
                prob = jnp.exp2(scores[tile] * (scale * LOG2E) - shift)
                if not (u or t):
                    prob = jnp.where(causal, prob, 0.0)
                halves.append(prob.astype(jnp.bfloat16))
                dscores.append((prob * (dprobs[tile] - delta[t]) * scale).astype(jnp.bfloat16))

        def square(tiles):
            return jnp.concatenate(
                [jnp.concatenate(tiles[:2], axis=1), jnp.concatenate(tiles[2:], axis=1)], axis=0
            )

        half, dscore = square(halves), square(dscores)
        for n, value in enumerate(
            (dot(dscore, keys, TN), dot(dscore, queries), dot(half, grads))
        ):
            acc[k, i, n] = value[:BLK]
            part[k, i, n] = value[BLK:].astype(jnp.bfloat16)

    def finish(k):
        f = [got_f.at[k + 1, s] for s in range(FWD)]
        b = [got_b.at[k + 1, s] for s in range(BACK)]
        back_f, back_b = far_f.at[k + 1], far_b.at[k + 1]

        def add(total, flag, value):
            value = value.astype(jnp.float32)
            return total + jnp.where(flag, value, jnp.zeros_like(value))

        p1l4_p2_p3 = either([p1l4, p2, p3])
        p2_p3 = either([p2, p3])
        p0g2_p1l4 = either([p0l4, p0s, p1l4])
        for i in range(4):
            here = cols(k, i)
            if i < 2:
                value = jnp.where(p2l4, b[4][i], f[2][i])
                total = add(acc[k, i, 0], p1l4_p2_p3, value)
            else:
                total = add(acc[k, i, 0], p2_p3, f[3][i - 2])
                total = add(total, p3, back_b[i - 2])
            dq_ref[:, here] = total.astype(jnp.bfloat16)
            for side, out in enumerate((dk_ref, dv_ref)):
                if i < 2:
                    value = jnp.where(p0l4, back_f[i, side], b[i][side])
                elif i == 2:
                    value = jnp.where(p1l4, b[4][side], b[3][side])
                else:
                    value = jnp.where(p1l4, f[3][side], b[4][side])
                out[:, here] = add(acc[k, i, 1 + side], p0g2_p1l4, value).astype(jnp.bfloat16)

    def period(k, final):
        ahead = k + 1
        if not final:
            post(ahead, 2, True)

            @pl.when(k < periods - 2)
            def _():
                start_pre(k + 2)

        fwd_copy(k, 0).wait_recv()
        back_copy(k, 0).wait_recv()
        compute(k, 0)
        if not final:
            wait_pre(ahead, range(4))
        post(ahead, 0, True, ins=not final)
        if not final:
            post(ahead, 0, False)
            post(ahead, 1, False)
        fwd_copy(k, 1).wait_recv()
        back_copy(k, 1).wait_recv()
        compute(k, 1)
        post(ahead, 1, True, ins=not final)
        post(ahead, 2, False, ins=not final)
        if final:
            direct_copy(0).start()
        fwd_copy(k, 2).wait_recv()
        back_copy(k, 2).wait_recv()
        compute(k, 2)
        if not final:
            post(ahead, 3, True)
        fwd_copy(k, 3).wait_recv()
        back_copy(k, 3).wait_recv()
        compute(k, 3)
        if final:
            direct_copy(1).start()
        post(ahead, 3, False, ins=not final)
        post(ahead, 4, True, ins=not final)
        if final:
            post(ahead, 3, True, ins=False)

    def forward_far(k):
        far_copy(k, 0).start()
        back_copy(k, 4).wait_recv()
        far_copy(k, 1).start()

    wait_pre(0, (2, 3))
    for s in range(4):
        post(0, s, False, outs=False)
    for copy in stat_copies:
        copy.wait_recv()

    def drain(k):
        for i in range(4):
            pre_copy(i, k).wait_send()
        for s in range(4):
            fwd_copy(k, s).wait_send()
            back_copy(k, s).wait_send()

        @pl.when(k > 0)
        def _():
            back_copy(k, 4).wait_send()
            for i in range(2):
                far_copy(k, i).wait_send()

    def step(k, carry):
        period(k, False)

        @pl.when(k > 0)
        def _():
            forward_far(k)
            drain(k - 1)

        @pl.when(k > 1)
        def _():
            for i in range(2):
                far_copy(k - 1, i).wait_recv()
            finish(k - 2)

        return carry

    lax.fori_loop(0, periods - 1, step, 0)
    end = periods - 1
    period(end, True)
    forward_far(end)
    for i in range(2):
        far_copy(end - 1, i).wait_recv()
    finish(end - 2)
    drain(end - 1)
    drain(end)
    for copy in count_copies + stat_copies:
        copy.wait_send()
    for i in range(2):
        far_copy(end, i).wait_recv()
    finish(end - 1)
    for s in (2, 3):
        fwd_copy(periods, s).wait_recv()
    for s in (0, 1, 3, 4):
        back_copy(periods, s).wait_recv()
    for i in range(2):
        direct_copy(i).wait_recv()
    finish(end)
    for s in (2, 3):
        fwd_copy(periods, s).wait_send()
    for s in (0, 1, 3, 4):
        back_copy(periods, s).wait_send()
    for i in range(2):
        direct_copy(i).wait_send()


def keep(a, b, c, a_out, b_out, c_out, sems):
    copies = [
        pltpu.make_async_copy(src, dst, sems.at[i])
        for i, (src, dst) in enumerate(((a, a_out), (b, b_out), (c, c_out)))
    ]
    for copy in copies:
        copy.start()
    for copy in copies:
        copy.wait()


def shards(blocks, q, k, v, g, lse, delta, counts):
    heads = lse.shape[0]
    periods = heads // 4
    rows, width = q.shape
    hbm = pl.BlockSpec(memory_space=pl.ANY)
    vmem = pl.BlockSpec(memory_space=pltpu.VMEM)
    grad = jax.ShapeDtypeStruct((rows, width), jnp.bfloat16)
    dma = pltpu.SemaphoreType.DMA

    def tiles(*lead, dtype=jnp.bfloat16):
        return pltpu.VMEM((*lead, BLK, DIM), dtype)

    grads = pl.pallas_call(
        functools.partial(kernel, blocks, heads),
        out_shape=(grad, grad, grad),
        in_specs=[hbm] * 6 + [pl.BlockSpec(memory_space=pltpu.SMEM)],
        out_specs=(vmem, vmem, vmem),
        scratch_shapes=[
            pltpu.VMEM((rows, width), jnp.bfloat16),
            pltpu.VMEM((rows, width), jnp.bfloat16),
            pltpu.VMEM((rows, width), jnp.bfloat16),
            pltpu.VMEM((rows, width), jnp.bfloat16),
            pltpu.VMEM((periods, 2, BLK, 2 * DIM), jnp.bfloat16),
            pltpu.VMEM((periods, 2, BLK, 2 * DIM), jnp.bfloat16),
            pltpu.VMEM((4, 2 * heads, BLK), jnp.float32),
            pltpu.VMEM((4, 8, BLK), jnp.float32),
            tiles(periods + 1, FWD, 2),
            tiles(periods + 1, BACK, 2),
            tiles(periods + 1, FWD, 2),
            tiles(periods + 1, BACK, 2),
            tiles(periods + 1, 2, 2),
            tiles(periods + 1, 2),
            tiles(periods, 4, 3, dtype=jnp.float32),
            tiles(periods, 4, 3),
            dma((6,)),
            dma((4,)),
            dma((4,)),
            dma((4,)),
            dma((4,)),
            dma((4, periods)),
            dma((4, periods)),
            dma((periods + 1, FWD)),
            dma((periods + 1, FWD)),
            dma((periods + 1, BACK)),
            dma((periods + 1, BACK)),
            dma((periods + 1, 2)),
            dma((periods + 1, 2)),
        ],
        compiler_params=pltpu.CompilerParams(
            collective_id=0, has_side_effects=True, vmem_limit_bytes=123 << 19
        ),
        cost_estimate=pl.CostEstimate(
            flops=40 * heads * BLK * BLK * DIM,
            bytes_accessed=14 * rows * width,
            transcendentals=4 * heads * BLK * BLK,
        ),
    )(q, k, v, g, lse, delta, counts)
    return pl.pallas_call(
        keep,
        out_shape=(grad, grad, grad),
        in_specs=[vmem] * 3,
        out_specs=(hbm, hbm, hbm),
        scratch_shapes=[pltpu.SemaphoreType.DMA((3,))],
        cost_estimate=pl.CostEstimate(
            flops=0, bytes_accessed=6 * rows * width, transcendentals=0
        ),
    )(*grads)


def solution(mesh):
    blocks = mesh.shape["seq"] * mesh.shape["pair"]
    rows = P(("seq", "pair"), None)
    cols = P(None, ("seq", "pair"))
    return jax.shard_map(
        functools.partial(shards, blocks),
        mesh=mesh,
        in_specs=(rows, rows, rows, rows, cols, cols, P(("seq", "pair"))),
        out_specs=(rows, rows, rows),
        check_vma=False,
    )
```

time: 300 us -> 67 us (0.22)
  the two profiles are of different devices: /device:TPU:506 before, /device:TPU:1 now
where the time goes in v3:
time: 67 us; the launch traced here: 66.9 us
  Pallas kernels  65.6 us (98%)
  between operations  1.29 us (2%)
    pallas_call x1, Pallas kernels, shards(): pl.pallas_call(functools.partial(kernel, blocks, heads), out_shape=(grad,...  62.8 us
    pallas_call x1, Pallas kernels, shards(): pl.pallas_call(keep, out_shape=(grad, grad, grad), in_specs=[vmem] * 3, o...  2.78 us

profile of v3, /device:TPU:1, one launch (start us, length us, event | category | flops | bytes accessed | tf_op | source)
XLA Modules:
  0.0 66.9 jit_solution(15757910237730531833)
XLA Ops:
  1.3 62.8 %shard_map.94 = (bf16[128,2560]{1,0:T(8,128)(2,1)}, bf16[128,2560]{1,0:T(8,128)(2,1)}, bf16[128,2560]{1,0:T(8,128)(2,1)}) custom-call(bf16[128,2560]{1,0:T(8,128)(2,1)} %q_hbm.1, bf16[128,2560]{1,0:T(8,128)(2,1)} %k_hbm.1, bf16[128,2560]{1,0:T(8,128)(2,1)} %v_hbm.1, bf16[128,2560]{1,0:T(8,128)(2,1)} %g_hbm.1, f32[20,128]{1,0:T(8,128)} %lse_hbm.1, ...), custom_call_target="tpu_custom_call" | custom-call | flops 1677721600 | bytes 4587520 | tf_op jit(solution)/shard_map/pallas_call | solution.py:489
  64.1 2.8 %shard_map.95 = (bf16[128,2560]{1,0:T(8,128)(2,1)}, bf16[128,2560]{1,0:T(8,128)(2,1)}, bf16[128,2560]{1,0:T(8,128)(2,1)}) custom-call(bf16[128,2560]{1,0:T(8,128)(2,1)} %get-tuple-element.6.a, bf16[128,2560]{1,0:T(8,128)(2,1)} %get-tuple-element.7.b, bf16[128,2560]{1,0:T(8,128)(2,1)} %get-tuple-element.8.c), custom_call_target="tpu_custom_call" | custom-call | bytes 1966080 | tf_op jit(solution)/shard_map/pallas_call | solution.py:534

commit v4 on v3

--- a/solution.py
+++ b/solution.py
@@ -100,58 +100,111 @@
     fetches = [
         pltpu.make_async_copy(lse_hbm, stats.at[0, pl.ds(0, heads)], fetch_sem.at[0]),
         pltpu.make_async_copy(delta_hbm, stats.at[0, pl.ds(heads, heads)], fetch_sem.at[1]),
-        pltpu.make_async_copy(k_hbm, k_own, fetch_sem.at[2]),
-        pltpu.make_async_copy(v_hbm, v_own, fetch_sem.at[3]),
-        pltpu.make_async_copy(q_hbm, q_own, fetch_sem.at[4]),
-        pltpu.make_async_copy(g_hbm, g_own, fetch_sem.at[5]),
     ]
+    operands = ((q_hbm, q_own), (g_hbm, g_own), (k_hbm, k_own), (v_hbm, v_own))
+    for n, columns in enumerate((pl.ds(0, 4 * DIM), pl.ds(4 * DIM, (heads - 4) * DIM))):
+        fetches += [
+            pltpu.make_async_copy(
+                hbm.at[:, columns], own.at[:, columns], fetch_sem.at[2 + 4 * n + i]
+            )
+            for i, (hbm, own) in enumerate(operands)
+        ]
     for fetch in fetches:
         fetch.start()
     counts[0] = jnp.full((8, BLK), cnt_ref[0], jnp.int32).astype(jnp.float32)
+    counts[1:] = jnp.ones((3, 8, BLK), jnp.float32)
+
+    def valid(offset):
+        return me < blocks - offset if offset > 0 else me >= -offset
+
+    def begin(copy, condition):
+        pl.when(condition)(copy.start)
+
+    def arrived(copy, condition):
+        pl.when(condition)(copy.wait_recv)
+
+    def sent(copy, condition):
+        pl.when(condition)(copy.wait_send)
+
+    at_first, at_third = me == 0, me == 3
+    at_last, at_head, ahead_of_head = (me == blocks - i for i in (1, 4, 5))
+
+    @pl.when(at_last)
+    def _():
+        stats[1] = jnp.zeros(stats.shape[1:], stats.dtype)
 
     barrier = pltpu.get_barrier_semaphore()
     for offset in (-1, 1, 2, 3, -3, -4, 4):
-        pl.semaphore_signal(barrier, 1, device_id=at(offset), device_id_type=MESH)
-    pl.semaphore_wait(barrier, 7)
+
+        @pl.when(valid(offset))
+        def _(offset=offset):
+            pl.semaphore_signal(barrier, 1, device_id=at(offset), device_id_type=MESH)
+
+    near = {3: (0,), 4: (1, blocks - 1), 5: (2, blocks - 2, blocks - 3), 6: (3, blocks - 4)}
+    for amount, places in near.items():
+
+        @pl.when(either([me == place for place in places]))
+        def _(amount=amount):
+            pl.semaphore_wait(barrier, amount)
+
+    @pl.when(both(me > 3, me < blocks - 4))
+    def _():
+        pl.semaphore_wait(barrier, 7)
+
+    def cols(k, i):
+        return pl.ds(pl.multiple_of((4 * k + i) * DIM, DIM), DIM)
+
+    def wide(k, first):
+        return pl.ds(pl.multiple_of((4 * k + first) * DIM, 2 * DIM), 2 * DIM)
+
+    def pre_copy(i, k, early=False):
+        own = ((k_hbm, v_hbm, q_hbm, g_hbm) if early else (k_own, v_own, q_own, g_own))[i]
+        src = own.at[:, wide(k, 0 if i < 2 else 2)]
+        dst = (kv_far if i < 2 else qg_far).at[k, i % 2]
+        return remote(src, dst, pre_send.at[i, k], pre_recv.at[i, k], 4 if i < 2 else -4)
+
+    def end_copies(i, k, early):
+        own = ((k_hbm, v_hbm, q_hbm, g_hbm) if early else (k_own, v_own, q_own, g_own))[i]
+        got, recv = (got_b, b_recv) if i < 2 else (got_f, f_recv)
+        return [
+            remote(
+                own.at[:, cols(k, s if i < 2 else 2 + s)],
+                got.at[k, s, i % 2],
+                pre_send.at[i, k],
+                recv.at[k, s],
+                3 if i < 2 else -3,
+            )
+            for s in range(2)
+        ]
+
+    def start_pre(k, early=False):
+        for i in range(4):
+            begin(pre_copy(i, k, early), valid(4 if i < 2 else -4))
+            for copy in end_copies(i, k, early):
+                begin(copy, at_head if i < 2 else at_third)
+
+    start_pre(0, True)
 
     count_copies = [
         remote(counts.at[0], counts.at[i], count_send.at[i], count_recv.at[i], -i)
         for i in (1, 2, 3)
     ]
-    for copy in count_copies:
-        copy.start()
+    for i, copy in enumerate(count_copies):
+        begin(copy, valid(-1 - i))
 
     stat_copies = [
         remote(stats.at[0], stats.at[i], stat_send.at[i], stat_recv.at[i], offset)
         for i, offset in ((1, -1), (2, 1), (3, -3))
     ]
-
     for fetch in fetches[:2]:
         fetch.wait()
-    for copy in stat_copies:
-        copy.start()
-
-    def wide(k, first):
-        return pl.ds(pl.multiple_of((4 * k + first) * DIM, 2 * DIM), 2 * DIM)
-
-    def pre_copy(i, k):
-        own = (k_own, v_own, q_own, g_own)[i]
-        src = own.at[:, wide(k, 0 if i < 2 else 2)]
-        dst = (kv_far if i < 2 else qg_far).at[k, i % 2]
-        return remote(src, dst, pre_send.at[i, k], pre_recv.at[i, k], 4 if i < 2 else -4)
-
-    def start_pre(k):
-        for i in range(4):
-            pre_copy(i, k).start()
-
-    for fetch in fetches[2:]:
+    stat_offsets = (-1, 1, -3)
+    for copy, offset in zip(stat_copies, stat_offsets):
+        begin(copy, valid(offset))
+    for fetch in fetches[2:6]:
         fetch.wait()
-    start_pre(0)
     place = cnt_ref[0]
     p0, p1, p2, p3 = (place == i for i in (1, 2, 3, 4))
-
-    def cols(k, i):
-        return pl.ds(pl.multiple_of((4 * k + i) * DIM, DIM), DIM)
 
     def content(kind, i, k, side):
         if kind == "kv":
@@ -187,6 +240,38 @@
         at_end = (far_send.at[periods, i], far_recv.at[periods, i])
         return remote(src, dst, *at_end, -3 if i == 0 else 3)
 
+    def end_far(k, i):
+        if i == 0:
+            src, dst = part.at[k - 1, pl.ds(0, 2), pl.ds(1, 2)], far_f.at[k]
+        else:
+            src, dst = part.at[k - 1, pl.ds(2, 2), 0], far_b.at[k]
+        send_sem = (f_send if i == 0 else b_send).at[k, 0]
+        return remote(src, dst, send_sem, far_recv.at[k, i], -3 if i == 0 else 3)
+
+    def sends_f():
+        return me < blocks - 1
+
+    def sends_b(s):
+        return both(me > 0, me != blocks - 4) if s in (2, 3) else me > 0
+
+    def wait_f(k, s):
+        arrived(fwd_copy(k, s), me > 0) if s in (2, 3) else fwd_copy(k, s).wait_recv()
+
+    def wait_b(k, s, flush=False):
+        if s in (2, 3):
+            arrived(back_copy(k, s), both(me < blocks - 1, me != blocks - 5))
+        elif s == 4 or flush:
+            arrived(back_copy(k, s), me < blocks - 1)
+        else:
+            back_copy(k, s).wait_recv()
+
+    def start_far(k, i):
+        begin(far_copy(k, i), valid((-4, 4)[i]))
+        begin(end_far(k, i), (at_last, at_first)[i])
+
+    def wait_far(k, i):
+        arrived(far_copy(k, i), (me < blocks - 3, me >= 3)[i])
+
     def send(table, k, s, back, ins=True, outs=True):
         stage = send_b if back else send_f
         table = [e for e in table if (ins and e[1][0] != "d") or (outs and e[1][0] == "d")]
@@ -195,21 +280,23 @@
             for flag, kind, i in table[:-1]:
                 value = jnp.where(flag, content(kind, i, k, side), value)
             stage[k, s, side] = value
-        (back_copy if back else fwd_copy)(k, s).start()
+        begin((back_copy if back else fwd_copy)(k, s), sends_b(s) if back else sends_f())
 
     def wait_pre(k, which):
         for i in which:
-            pre_copy(i, k).wait_recv()
-
-    send(((p1, "kv", 3), (None, "qg", 2)), 0, 2, True)
+            arrived(pre_copy(i, k), valid(-4 if i < 2 else 4))
+
+    def send_2(k):
+        send(((p1, "kv", 3), (None, "qg", 2)), k, 2, True)
+
+    send_2(0)
     send(((None, "qg", 3),), 0, 3, True)
+    for fetch in fetches[6:]:
+        fetch.wait()
+    send_2(1)
     start_pre(1)
-    wait_pre(0, (0, 1))
-    for s in range(2):
-        send(((p0, "kvx", s), (None, "qg", s)), 0, s, True)
-
-    for copy in count_copies:
-        copy.wait_recv()
+    for i, copy in enumerate(count_copies):
+        arrived(copy, valid(1 + i))
     c1, c2, c3 = (jnp.max(counts[i]) for i in (1, 2, 3))
     p0l4 = both(p0, c3 == 4.0)
     p1l4 = both(p1, c2 == 4.0)
@@ -354,113 +441,138 @@
                     value = jnp.where(p1l4, f[3][side], b[4][side])
                 out[:, here] = add(acc[k, i, 1 + side], p0g2_p1l4, value).astype(jnp.bfloat16)
 
+    def forward_back(k):
+        wait_b(k, 4)
+        start_far(k, 1)
+
     def period(k, final):
         ahead = k + 1
         if not final:
-            post(ahead, 2, True)
-
-            @pl.when(k < periods - 2)
+
+            @pl.when(k < periods - 3)
             def _():
-                start_pre(k + 2)
-
-        fwd_copy(k, 0).wait_recv()
-        back_copy(k, 0).wait_recv()
+                start_pre(k + 3)
+
+        wait_f(k, 0)
+        wait_b(k, 0)
         compute(k, 0)
         if not final:
-            wait_pre(ahead, range(4))
+            wait_pre(ahead, (0, 1))
         post(ahead, 0, True, ins=not final)
-        if not final:
-            post(ahead, 0, False)
-            post(ahead, 1, False)
-        fwd_copy(k, 1).wait_recv()
-        back_copy(k, 1).wait_recv()
+        wait_f(k, 1)
+        wait_b(k, 1)
         compute(k, 1)
         post(ahead, 1, True, ins=not final)
         post(ahead, 2, False, ins=not final)
         if final:
-            direct_copy(0).start()
-        fwd_copy(k, 2).wait_recv()
-        back_copy(k, 2).wait_recv()
+            begin(direct_copy(0), valid(-3))
+
+        @pl.when(k > 1)
+        def _():
+            forward_back(k - 1)
+
+        wait_f(k, 2)
+        wait_b(k, 2)
         compute(k, 2)
         if not final:
             post(ahead, 3, True)
-        fwd_copy(k, 3).wait_recv()
-        back_copy(k, 3).wait_recv()
+
+            @pl.when(k < periods - 2)
+            def _():
+                wait_pre(k + 2, (2, 3))
+                post(k + 2, 0, False)
+                post(k + 2, 1, False)
+
+        wait_f(k, 3)
+        wait_b(k, 3)
         compute(k, 3)
         if final:
-            direct_copy(1).start()
+            begin(direct_copy(1), valid(3))
         post(ahead, 3, False, ins=not final)
         post(ahead, 4, True, ins=not final)
         if final:
             post(ahead, 3, True, ins=False)
 
-    def forward_far(k):
-        far_copy(k, 0).start()
-        back_copy(k, 4).wait_recv()
-        far_copy(k, 1).start()
-
-    wait_pre(0, (2, 3))
-    for s in range(4):
+    wait_pre(0, range(4))
+    for s in range(2):
+        post(0, s, True, outs=False)
         post(0, s, False, outs=False)
-    for copy in stat_copies:
-        copy.wait_recv()
+    for s in (2, 3):
+        post(0, s, False, outs=False)
+    start_pre(2)
+    for k in range(2, periods):
+        send_2(k)
+    wait_pre(1, (2, 3))
+    post(1, 0, False)
+    post(1, 1, False)
+    for copy, offset in zip(stat_copies, stat_offsets):
+        arrived(copy, valid(-offset))
 
     def drain(k):
-        for i in range(4):
-            pre_copy(i, k).wait_send()
+        for i in range(2):
+            sent(pre_copy(i, k), either([valid(4), at_head]))
+            sent(pre_copy(2 + i, k), either([valid(-4), at_third]))
         for s in range(4):
-            fwd_copy(k, s).wait_send()
-            back_copy(k, s).wait_send()
+            sent(fwd_copy(k, s), sends_f())
+            sent(back_copy(k, s), sends_b(s))
 
         @pl.when(k > 0)
         def _():
-            back_copy(k, 4).wait_send()
+            sent(back_copy(k, 4), sends_b(4))
             for i in range(2):
-                far_copy(k, i).wait_send()
+                sent(far_copy(k, i), valid((-4, 4)[i]))
+                sent(end_far(k, i), (at_last, at_first)[i])
+
+    def finish_far(k):
+        for i in range(2):
+            wait_far(k + 1, i)
+        finish(k)
 
     def step(k, carry):
         period(k, False)
 
         @pl.when(k > 0)
         def _():
-            forward_far(k)
-            drain(k - 1)
+            start_far(k, 0)
 
         @pl.when(k > 1)
         def _():
-            for i in range(2):
-                far_copy(k - 1, i).wait_recv()
-            finish(k - 2)
+            drain(k - 2)
+
+        @pl.when(k > 2)
+        def _():
+            finish_far(k - 3)
 
         return carry
 
     lax.fori_loop(0, periods - 1, step, 0)
     end = periods - 1
     period(end, True)
-    forward_far(end)
+    start_far(end, 0)
+    finish_far(end - 3)
+    forward_back(end)
+    finish_far(end - 2)
+    for k in range(end - 2, end):
+        drain(k)
+    for i, copy in enumerate(count_copies):
+        sent(copy, valid(-1 - i))
+    for copy, offset in zip(stat_copies, stat_offsets):
+        sent(copy, valid(offset))
+    finish_far(end - 1)
+    drain(end)
+    for s in (2, 3):
+        wait_f(periods, s)
+    for s in (0, 1, 3, 4):
+        wait_b(periods, s, True)
     for i in range(2):
-        far_copy(end - 1, i).wait_recv()
-    finish(end - 2)
-    drain(end - 1)
-    drain(end)
-    for copy in count_copies + stat_copies:
-        copy.wait_send()
-    for i in range(2):
-        far_copy(end, i).wait_recv()
-    finish(end - 1)
-    for s in (2, 3):
-        fwd_copy(periods, s).wait_recv()
-    for s in (0, 1, 3, 4):
-        back_copy(periods, s).wait_recv()
-    for i in range(2):
-        direct_copy(i).wait_recv()
+        arrived(direct_copy(i), (me < blocks - 3, me >= 3)[i])
     finish(end)
     for s in (2, 3):
-        fwd_copy(periods, s).wait_send()
+        sent(fwd_copy(periods, s), sends_f())
     for s in (0, 1, 3, 4):
-        back_copy(periods, s).wait_send()
+        sent(back_copy(periods, s), sends_b(s))
     for i in range(2):
-        direct_copy(i).wait_send()
+        sent(direct_copy(i), valid((-3, 3)[i]))
 
 
 def keep(a, b, c, a_out, b_out, c_out, sems):
@@ -508,7 +620,7 @@
             tiles(periods + 1, 2),
             tiles(periods, 4, 3, dtype=jnp.float32),
             tiles(periods, 4, 3),
-            dma((6,)),
+            dma((10,)),
             dma((4,)),
             dma((4,)),
             dma((4,)),

time: 67 us -> 61.3 us (0.915)
  Pallas kernels: 65.6 us -> 59.8 us
    pallas_call x1, Pallas kernels: 62.8 us -> 57 us  [shards(): pl.pallas_call(functools.partial(kernel, blocks, heads), out_shape=(grad,...]
where the time goes in v4:
time: 61.3 us; the launch traced here: 61.1 us
  Pallas kernels  59.8 us (98%)
  between operations  1.29 us (2%)
    pallas_call x1, Pallas kernels, shards(): pl.pallas_call(functools.partial(kernel, blocks, heads), out_shape=(grad,...  57 us
    pallas_call x1, Pallas kernels, shards(): pl.pallas_call(keep, out_shape=(grad, grad, grad), in_specs=[vmem] * 3, o...  2.78 us

profile of v4, /device:TPU:1, one launch (start us, length us, event | category | flops | bytes accessed | tf_op | source)
XLA Modules:
  0.0 61.1 jit_solution(6020409200578336959)
XLA Ops:
  1.3 57.0 %shard_map.94 = (bf16[128,2560]{1,0:T(8,128)(2,1)}, bf16[128,2560]{1,0:T(8,128)(2,1)}, bf16[128,2560]{1,0:T(8,128)(2,1)}) custom-call(bf16[128,2560]{1,0:T(8,128)(2,1)} %q_hbm.1, bf16[128,2560]{1,0:T(8,128)(2,1)} %k_hbm.1, bf16[128,2560]{1,0:T(8,128)(2,1)} %v_hbm.1, bf16[128,2560]{1,0:T(8,128)(2,1)} %g_hbm.1, f32[20,128]{1,0:T(8,128)} %lse_hbm.1, ...), custom_call_target="tpu_custom_call" | custom-call | flops 1677721600 | bytes 4587520 | tf_op jit(solution)/shard_map/pallas_call | solution.py:601
  58.3 2.8 %shard_map.95 = (bf16[128,2560]{1,0:T(8,128)(2,1)}, bf16[128,2560]{1,0:T(8,128)(2,1)}, bf16[128,2560]{1,0:T(8,128)(2,1)}) custom-call(bf16[128,2560]{1,0:T(8,128)(2,1)} %get-tuple-element.6.a, bf16[128,2560]{1,0:T(8,128)(2,1)} %get-tuple-element.7.b, bf16[128,2560]{1,0:T(8,128)(2,1)} %get-tuple-element.8.c), custom_call_target="tpu_custom_call" | custom-call | bytes 1966080 | tf_op jit(solution)/shard_map/pallas_call | solution.py:646

commit v5 on v4

--- a/solution.py
+++ b/solution.py
@@ -45,9 +45,13 @@
     lse_hbm,
     delta_hbm,
     cnt_ref,
+    dq_hbm,
+    dk_hbm,
+    dv_hbm,
     dq_ref,
     dk_ref,
     dv_ref,
+    out_sem,
     q_own,
     k_own,
     v_own,
@@ -411,6 +415,15 @@
             acc[k, i, n] = value[:BLK]
             part[k, i, n] = value[BLK:].astype(jnp.bfloat16)
 
+    def out_copies(k):
+        columns = pl.ds(pl.multiple_of(4 * k * DIM, 4 * DIM), 4 * DIM)
+        return [
+            pltpu.make_async_copy(ref.at[:, columns], hbm.at[:, columns], out_sem.at[n, k])
+            for n, (ref, hbm) in enumerate(
+                ((dq_ref, dq_hbm), (dk_ref, dk_hbm), (dv_ref, dv_hbm))
+            )
+        ]
+
     def finish(k):
         f = [got_f.at[k + 1, s] for s in range(FWD)]
         b = [got_b.at[k + 1, s] for s in range(BACK)]
@@ -440,6 +453,8 @@
                 else:
                     value = jnp.where(p1l4, f[3][side], b[4][side])
                 out[:, here] = add(acc[k, i, 1 + side], p0g2_p1l4, value).astype(jnp.bfloat16)
+        for copy in out_copies(k):
+            copy.start()
 
     def forward_back(k):
         wait_b(k, 4)
@@ -573,17 +588,29 @@
         sent(back_copy(periods, s), sends_b(s))
     for i in range(2):
         sent(direct_copy(i), valid((-3, 3)[i]))
-
-
-def keep(a, b, c, a_out, b_out, c_out, sems):
-    copies = [
-        pltpu.make_async_copy(src, dst, sems.at[i])
-        for i, (src, dst) in enumerate(((a, a_out), (b, b_out), (c, c_out)))
-    ]
-    for copy in copies:
-        copy.start()
-    for copy in copies:
-        copy.wait()
+    for k in range(periods):
+        for copy in out_copies(k):
+            copy.wait()
+
+
+def keep(a, b, c, a_out, b_out, c_out, held, in_sem, out_sem):
+    pairs = []
+    for half in range(2):
+        rows = pl.ds(half * (BLK // 2), BLK // 2)
+        for i, (src, dst) in enumerate(((a, a_out), (b, b_out), (c, c_out))):
+            pairs.append(
+                (
+                    pltpu.make_async_copy(src.at[rows], held.at[i, rows], in_sem.at[half, i]),
+                    pltpu.make_async_copy(held.at[i, rows], dst.at[rows], out_sem.at[half, i]),
+                )
+            )
+    for fetch, _ in pairs:
+        fetch.start()
+    for fetch, write in pairs:
+        fetch.wait()
+        write.start()
+    for _, write in pairs:
+        write.wait()
 
 
 def shards(blocks, q, k, v, g, lse, delta, counts):
@@ -591,7 +618,6 @@
     periods = heads // 4
     rows, width = q.shape
     hbm = pl.BlockSpec(memory_space=pl.ANY)
-    vmem = pl.BlockSpec(memory_space=pltpu.VMEM)
     grad = jax.ShapeDtypeStruct((rows, width), jnp.bfloat16)
     dma = pltpu.SemaphoreType.DMA
 
@@ -602,8 +628,12 @@
         functools.partial(kernel, blocks, heads),
         out_shape=(grad, grad, grad),
         in_specs=[hbm] * 6 + [pl.BlockSpec(memory_space=pltpu.SMEM)],
-        out_specs=(vmem, vmem, vmem),
+        out_specs=(hbm, hbm, hbm),
         scratch_shapes=[
+            pltpu.VMEM((rows, width), jnp.bfloat16),
+            pltpu.VMEM((rows, width), jnp.bfloat16),
+            pltpu.VMEM((rows, width), jnp.bfloat16),
+            dma((3, periods)),
             pltpu.VMEM((rows, width), jnp.bfloat16),
             pltpu.VMEM((rows, width), jnp.bfloat16),
             pltpu.VMEM((rows, width), jnp.bfloat16),
@@ -646,9 +676,10 @@
     return pl.pallas_call(
         keep,
         out_shape=(grad, grad, grad),
-        in_specs=[vmem] * 3,
+        in_specs=[hbm] * 3,
         out_specs=(hbm, hbm, hbm),
-        scratch_shapes=[pltpu.SemaphoreType.DMA((3,))],
+        scratch_shapes=[pltpu.VMEM((3, rows, width), jnp.bfloat16), dma((2, 3)), dma((2, 3))],
+        compiler_params=pltpu.CompilerParams(vmem_limit_bytes=123 << 19),
         cost_estimate=pl.CostEstimate(
             flops=0, bytes_accessed=6 * rows * width, transcendentals=0
         ),

time: 61.3 us -> 60.4 us (0.985)
  Pallas kernels: 59.8 us -> 58.9 us
where the time goes in v5:
time: 60.4 us; the launch traced here: 60.2 us
  Pallas kernels  58.9 us (98%)
  between operations  1.29 us (2%)
    pallas_call x1, Pallas kernels, shards(): pl.pallas_call(functools.partial(kernel, blocks, heads), out_shape=(grad,...  56.6 us
    pallas_call x1, Pallas kernels, shards(): pl.pallas_call(keep, out_shape=(grad, grad, grad), in_specs=[hbm] * 3, ou...  2.34 us

profile of v5, /device:TPU:1, one launch (start us, length us, event | category | flops | bytes accessed | tf_op | source)
XLA Modules:
  0.0 60.2 jit_solution(15271959166925947162)
XLA Ops:
  1.3 56.6 %shard_map.94 = (bf16[128,2560]{1,0:T(8,128)(2,1)}, bf16[128,2560]{1,0:T(8,128)(2,1)}, bf16[128,2560]{1,0:T(8,128)(2,1)}) custom-call(bf16[128,2560]{1,0:T(8,128)(2,1)} %q_hbm.1, bf16[128,2560]{1,0:T(8,128)(2,1)} %k_hbm.1, bf16[128,2560]{1,0:T(8,128)(2,1)} %v_hbm.1, bf16[128,2560]{1,0:T(8,128)(2,1)} %g_hbm.1, f32[20,128]{1,0:T(8,128)} %lse_hbm.1, ...), custom_call_target="tpu_custom_call" | custom-call | flops 1677721600 | bytes 4587520 | tf_op jit(solution)/shard_map/pallas_call | solution.py:627
  57.8 2.3 %shard_map.95 = (bf16[128,2560]{1,0:T(8,128)(2,1)}, bf16[128,2560]{1,0:T(8,128)(2,1)}, bf16[128,2560]{1,0:T(8,128)(2,1)}) custom-call(bf16[128,2560]{1,0:T(8,128)(2,1)} %get-tuple-element.6.a, bf16[128,2560]{1,0:T(8,128)(2,1)} %get-tuple-element.7.b, bf16[128,2560]{1,0:T(8,128)(2,1)} %get-tuple-element.8.c), custom_call_target="tpu_custom_call" | custom-call | bytes 1966080 | tf_op jit(solution)/shard_map/pallas_call | solution.py:676
